TPU v7x, 256 devices: a whole 4x4x8 slice. The times are simulated.
256 devices in a mesh: ctx: 64 (over y, z, x_lo), head: 4 (over x_hi, core).
Axes of the slice: x: 4 (x_hi: 2, x_lo: 2; x = x_hi * 2 + x_lo), y: 4, z: 8, core: 2. Of those that a mesh axis runs over, the one named last changes fastest.
Arguments:
- queries: bfloat16 [8192, 64, 576], P('ctx', 'head'), may hold values from -22 to 22
- latent_kv: bfloat16 [8192, 576], P('ctx'), may hold values from -22 to 22
- positions: int32 [8192], P('ctx'), may hold values from 0 to 896, as said below
- value_up: bfloat16 [512, 64, 128], P(None, 'head'), may hold values from -0.25 to 0.25
- cotangent: bfloat16 [8192, 64, 128], P('ctx', 'head'), may hold values from -6 to 6
Outputs:
- attn_out: bfloat16 [8192, 64, 128], P('ctx', 'head')
- grad_queries: bfloat16 [8192, 64, 576], P('ctx', 'head')
- grad_latent: bfloat16 [8192, 576], P('ctx')
- grad_value_up: float32 [512, 64, 128], P('ctx', 'head')
Inputs may be any that keep to these rules, and one draw needn't show every extreme that they name: `positions`: positions count up by one inside a document and are 0 where a document begins; no document holds more than 897 tokens, and some document holds exactly 897.
All inputs are finite; a program needn't handle non-finite values.
Results may differ from a plain program's by a relative error of at most 0.02.
The roundings to bfloat16 on the way count: a program that leaves them out, or rounds other values in their place, can miss the bound.
Values may be sent and summed in bfloat16 or wider, within the bound.
A program may use at most 320 MiB of HBM per device.

v0:
```python
import math

import jax
import jax.numpy as jnp
from jax import lax
from jax.sharding import PartitionSpec as P

D_C = 512
D_R = 64
D_NOPE = 128
REACH = 8


ROPE_BASE = 10000.0


def shifted(value, axis, by):
    peers = lax.axis_size(axis)
    pairs = [(i, i + by) for i in range(peers) if 0 <= i + by < peers]
    return lax.ppermute(value, axis, pairs)


def shortened(value):

    def short(part):
        return part.astype(jnp.bfloat16) if part.dtype == jnp.float32 else part

    return jax.tree.map(short, value)


def rope_tables(positions):
    half_dim = D_R // 2
    frequency = ROPE_BASE ** (-2.0 * jnp.arange(half_dim, dtype=jnp.float32) / D_R)
    angles = positions.astype(jnp.float32)[:, None] * frequency[None, :]
    return (jnp.cos(angles), jnp.sin(angles))


def rotate(vectors, cosine_table, sine_table):
    half_dim = vectors.shape[-1] // 2
    lower_half = vectors[..., :half_dim]
    upper_half = vectors[..., half_dim:]
    return jnp.concatenate(
        [
            lower_half * cosine_table - upper_half * sine_table,
            upper_half * cosine_table + lower_half * sine_table,
        ],
        axis=-1,
    )


def unrotate(gradients, cosine_table, sine_table):
    half_dim = gradients.shape[-1] // 2
    lower_half = gradients[..., :half_dim]
    upper_half = gradients[..., half_dim:]
    return jnp.concatenate(
        [
            lower_half * cosine_table + upper_half * sine_table,
            upper_half * cosine_table - lower_half * sine_table,
        ],
        axis=-1,
    )


def guarded(visible, work, blank, *operands):
    return work(*operands)


def body(queries, latent_kv, positions, value_up, cotangent):
    tok_count = queries.shape[0]
    local_heads = queries.shape[1]
    kv_width = latent_kv.shape[1]
    softmax_scale = 1.0 / math.sqrt(D_NOPE + D_R)
    device_at = lax.axis_index("ctx")
    cosine_table, sine_table = rope_tables(positions)
    q_rope = rotate(
        queries[:, :, D_C:].astype(jnp.float32), cosine_table[:, None, :], sine_table[:, None, :]
    ).astype(jnp.bfloat16)
    q_cat = jnp.concatenate([queries[:, :, :D_C], q_rope], axis=-1)
    k_rope = rotate(latent_kv[:, D_C:].astype(jnp.float32), cosine_table, sine_table).astype(
        jnp.bfloat16
    )
    k_cat = jnp.concatenate([latent_kv[:, :D_C], k_rope], axis=-1)
    offsets = jnp.arange(tok_count, dtype=jnp.int32)
    q_global = device_at * tok_count + offsets
    q_begin = q_global - positions
    blocks = [(k_cat, q_begin)]
    moving = (k_cat, q_begin)
    for stride in range(1, REACH):
        moving = shifted((moving[0], moving[1]), "ctx", 1)
        blocks.append(moving)
    visible_masks = []
    for stride in range(REACH):
        k_global = (device_at - stride) * tok_count + offsets
        visible_masks.append(
            (k_global[None, :] <= q_global[:, None])
            & (k_global[None, :] >= 0)
            & (blocks[stride][1][None, :] == q_begin[:, None])
        )

    def tile_scores(k_block, visible):
        raw_scores = (
            jnp.einsum("qhd,kd->hqk", q_cat, k_block, preferred_element_type=jnp.float32)
            * softmax_scale
        )
        return jnp.where(visible[None], raw_scores, -jnp.inf)

    masked_tile = jnp.full((local_heads, tok_count, tok_count), -jnp.inf, jnp.float32)
    score_tiles = [
        guarded(
            visible_masks[stride],
            tile_scores,
            masked_tile,
            blocks[stride][0],
            visible_masks[stride],
        )
        for stride in range(REACH)
    ]
    row_peak = jnp.max(score_tiles[0], axis=2, keepdims=True)
    for score_tile in score_tiles[1:]:
        row_peak = jnp.maximum(row_peak, jnp.max(score_tile, axis=2, keepdims=True))
    row_mass = jnp.zeros_like(row_peak)
    for score_tile in score_tiles:
        row_mass = row_mass + jnp.sum(jnp.exp(score_tile - row_peak), axis=2, keepdims=True)
    log_total = row_peak + jnp.log(row_mass)
    prob_tiles = [
        jnp.exp(score_tile - log_total).astype(jnp.bfloat16) for score_tile in score_tiles
    ]

    def value_sum(prob_tile, k_block):
        return jnp.einsum(
            "hqk,kc->hqc", prob_tile, k_block[:, :D_C], preferred_element_type=jnp.float32
        )

    zero_latent = jnp.zeros((local_heads, tok_count, D_C), jnp.float32)
    o_sum = zero_latent
    for stride in range(REACH):
        o_sum = o_sum + guarded(
            visible_masks[stride], value_sum, zero_latent, prob_tiles[stride], blocks[stride][0]
        )
    o_lat = o_sum.astype(jnp.bfloat16)
    attn_out = jnp.einsum(
        "hqc,chv->qhv", o_lat, value_up, preferred_element_type=jnp.float32
    ).astype(jnp.bfloat16)
    do_lat = jnp.einsum(
        "qhv,chv->hqc", cotangent, value_up, preferred_element_type=jnp.float32
    ).astype(jnp.bfloat16)

    def prob_grads(k_block):
        return jnp.einsum(
            "hqc,kc->hqk", do_lat, k_block[:, :D_C], preferred_element_type=jnp.float32
        )

    zero_tile = jnp.zeros((local_heads, tok_count, tok_count), jnp.float32)
    dp_tiles = [
        guarded(visible_masks[stride], prob_grads, zero_tile, blocks[stride][0])
        for stride in range(REACH)
    ]
    row_delta = jnp.zeros_like(row_peak)
    for stride in range(REACH):
        row_delta = row_delta + jnp.sum(
            prob_tiles[stride].astype(jnp.float32) * dp_tiles[stride], axis=2, keepdims=True
        )

    def block_grads(k_block, prob_tile, dp_tile):
        d_scores = (prob_tile.astype(jnp.float32) * (dp_tile - row_delta) * softmax_scale).astype(
            jnp.bfloat16
        )
        dq_part = jnp.einsum("hqk,kd->qhd", d_scores, k_block, preferred_element_type=jnp.float32)
        d_key = jnp.einsum("hqk,qhd->kd", d_scores, q_cat, preferred_element_type=jnp.float32)
        d_value = jnp.einsum("hqk,hqc->kc", prob_tile, do_lat, preferred_element_type=jnp.float32)
        return (dq_part, jnp.concatenate([d_key[:, :D_C] + d_value, d_key[:, D_C:]], axis=1))

    zero_query = jnp.zeros((tok_count, local_heads, kv_width), jnp.float32)
    zero_key = jnp.zeros((tok_count, kv_width), jnp.float32)
    dq_sum = zero_query
    key_grads = []
    for stride in range(REACH):
        dq_part, key_part = guarded(
            visible_masks[stride],
            block_grads,
            (zero_query, zero_key),
            blocks[stride][0],
            prob_tiles[stride],
            dp_tiles[stride],
        )
        dq_sum = dq_sum + dq_part
        key_grads.append(key_part)
    returned = jnp.zeros((tok_count, kv_width), jnp.float32)
    for stride in range(REACH - 1, 0, -1):
        returned = shifted(shortened(returned + key_grads[stride]), "ctx", -1)
    summed = lax.psum(returned + key_grads[0], "head")
    grad_latent = jnp.concatenate(
        [summed[:, :D_C], unrotate(summed[:, D_C:], cosine_table, sine_table)], axis=1
    ).astype(jnp.bfloat16)
    grad_queries = jnp.concatenate(
        [
            dq_sum[:, :, :D_C],
            unrotate(dq_sum[:, :, D_C:], cosine_table[:, None, :], sine_table[:, None, :]),
        ],
        axis=-1,
    ).astype(jnp.bfloat16)
    grad_value_up = lax.psum_scatter(
        jnp.einsum("hqc,qhv->chv", o_lat, cotangent, preferred_element_type=jnp.float32),
        "ctx",
        scatter_dimension=0,
        tiled=True,
    )
    return (attn_out, grad_queries, grad_latent, grad_value_up)


def solution(mesh):
    in_specs = (
        P("ctx", "head", None),
        P("ctx", None),
        P("ctx"),
        P(None, "head", None),
        P("ctx", "head", None),
    )
    out_specs = (
        P("ctx", "head", None),
        P("ctx", "head", None),
        P("ctx", None),
        P("ctx", "head", None),
    )
    return jax.shard_map(body, mesh=mesh, in_specs=in_specs, out_specs=out_specs, check_vma=False)
```

profile of v0, /device:TPU:2, one launch (start us, length us, event | category | flops | bytes accessed | tf_op | source)
XLA Modules:
  0.0 577.1 jit_solution(18406156026976573962)
XLA Ops:
  8.9 3.8 collective-permute-start
  14.5 3.4 collective-permute-start.1
  19.0 3.7 convolution_convert_fusion
  23.5 3.8 collective-permute-start.2
  27.3 1.6 collective-permute-done.2
  28.9 4.7 collective-permute-start.4
  33.6 1.3 collective-permute-done.4
  34.9 5.0 collective-permute-start.6
  40.0 1.3 collective-permute-done.6
  41.2 5.0 collective-permute-start.8
  46.3 1.8 slice.131
  48.1 4.5 collective-permute-start.10
  53.9 5.0 collective-permute-start.12
  60.4 5.1 collective-permute-start.3
  66.9 1.2 collective-permute-done.3
  68.1 5.3 collective-permute-start.5
  74.8 1.2 collective-permute-done.5
  76.0 5.3 collective-permute-start.7
  82.8 1.2 collective-permute-done.7
  83.9 5.3 collective-permute-start.9
  90.7 1.2 collective-permute-done.9
  91.9 5.3 collective-permute-start.11
  98.6 1.2 collective-permute-done.11
  99.8 5.7 collective-permute-start.13
  108.4 1.9 exponential_reduce_fusion.6
  110.4 1.9 fusion.27
  112.3 2.4 fusion.48
  114.8 4.6 fusion.50
  122.6 2.1 collective-permute-start.14
  125.5 1.6 fusion.24
  127.9 1.6 fusion.22
  130.3 1.6 fusion.20
  131.9 1.5 convolution_bitcast_fusion.7
  135.4 2.7 fusion.93
  138.1 2.8 fusion.91
  140.9 2.8 fusion.89
  143.7 2.7 fusion.87
  146.4 9.3 %add_convert_fusion = bf16[16,128,512]{2,1,0:T(8,128)(2,1)} fusion(f32[16,128,512]{2,1,0:T(8,128)S(1)} %fusion.97, f32[16,128,512]{2,1,0:T(8,128)S(1)} %fusion.95, f32[16,128,512]{2,1,0:T(8,128)} %fusion.93, f32[16,128,512]{2,1,0:T(8,128)} %fusion.91, f32[16,128,512]{2,1,0:T(8,128)} %fusion.89, f32[16,128,512]{2,1,0:T(8,128)S(1)} %fusion.84, ...), kind=kOutput, calls=%fused_computation.2 | convolution fusion | flops 276824064 | bytes 32112640 | tf_op jit(solution)/shard_map/hqk,kc->hqc/dot_general | solution.py:130
  155.7 2.0 fusion.19
  158.6 1.9 collective-permute-start.15
  161.4 5.6 collective-permute-done.15
  167.1 1.9 collective-permute-start.16
  169.9 5.4 collective-permute-done.16
  175.3 2.1 collective-permute-start.17
  178.3 6.7 %collective-permute-done.17 = bf16[128,576]{0,1:T(8,128)(2,1)S(1)} collective-permute-done((bf16[128,576]{0,1:T(8,128)(2,1)S(1)}, bf16[128,576]{0,1:T(8,128)(2,1)S(1)}, u32[]{:S(2)}, u32[]{:S(2)}) %collective-permute-start.17) | collective-permute-done | bytes 147488 | tf_op jit(solution)/shard_map/ppermute | solution.py:20
  185.0 1.9 collective-permute-start.18
  187.8 7.8 %collective-permute-done.18 = bf16[128,576]{0,1:T(8,128)(2,1)S(1)} collective-permute-done((bf16[128,576]{0,1:T(8,128)(2,1)S(1)}, bf16[128,576]{0,1:T(8,128)(2,1)S(1)}, u32[]{:S(2)}, u32[]{:S(2)}) %collective-permute-start.18) | collective-permute-done | bytes 147488 | tf_op jit(solution)/shard_map/ppermute | solution.py:20
  195.6 1.9 collective-permute-start.19
  198.4 7.5 %collective-permute-done.19 = bf16[128,576]{0,1:T(8,128)(2,1)S(1)} collective-permute-done((bf16[128,576]{0,1:T(8,128)(2,1)S(1)}, bf16[128,576]{0,1:T(8,128)(2,1)S(1)}, u32[]{:S(2)}, u32[]{:S(2)}) %collective-permute-start.19) | collective-permute-done | bytes 147488 | tf_op jit(solution)/shard_map/ppermute | solution.py:20
  205.9 1.9 collective-permute-start.20
  208.8 7.6 %collective-permute-done.20 = bf16[128,576]{0,1:T(8,128)(2,1)S(1)} collective-permute-done((bf16[128,576]{0,1:T(8,128)(2,1)S(1)}, bf16[128,576]{0,1:T(8,128)(2,1)S(1)}, u32[]{:S(2)}, u32[]{:S(2)}) %collective-permute-start.20) | collective-permute-done | bytes 147488 | tf_op jit(solution)/shard_map/ppermute | solution.py:20
  217.3 4.4 convolution_bitcast_fusion
  221.7 2.8 fusion.15
  224.6 1.1 copy.62
  228.8 2.9 fusion.70
  231.7 2.9 fusion.67
  234.7 3.0 fusion.64
  237.7 2.9 fusion.61
  240.6 10.9 %add_bitcast_fusion = f32[128,16,576]{0,2,1:T(8,128)} fusion(f32[576,16,128]{2,0,1:T(8,128)} %fusion.61, f32[576,16,128]{2,0,1:T(8,128)} %fusion.64, f32[576,16,128]{2,0,1:T(8,128)} %fusion.67, f32[576,16,128]{2,0,1:T(8,128)} %fusion.70, f32[576,16,128]{2,0,1:T(8,128)S(1)} %fusion.73, f32[576,16,128]{2,0,1:T(8,128)S(1)} %fusion.79, ...), kind=kOutput, calls=%fused_computation | convolution fusion | flops 310247424 | bytes 38420480 | tf_op jit(solution)/shard_map/hqk,kd->qhd/dot_general | solution.py:168
  251.5 2.6 slice.255
  255.2 1.6 pad_maximum_fusion.1
  256.8 35.3 %all-reduce.2.cloned.1.call-done = f32[128,576]{0,1:T(8,128)} async-done(((f32[128,576]{0,1:T(8,128)}), f32[128,576]{0,1:T(8,128)}) %all-reduce.2.cloned.1.call-update) | async-done | bytes 294928 | tf_op jit(solution)/shard_map/psum | solution.py:191
  294.7 273.3 %reduce-scatter.2.cloned.1.call-done = f32[8,16,128]{2,0,1:T(8,128)} async-done(((f32[512,16,128]{2,0,1:T(8,128)}), f32[8,16,128]{2,0,1:T(8,128)}) %reduce-scatter.2.cloned.1.call-update) | async-done | bytes 65552 | tf_op jit(solution)/shard_map/reduce_scatter | solution.py:202
  567.9 1.5 copy.63
  (230 shorter events, 38.4 us)
Async XLA Ops:
  8.0 11.0 %copy-start = (bf16[512,16,128]{2,1,0:T(8,128)(2,1)S(1)}, bf16[512,16,128]{2,1,0:T(8,128)(2,1)}, u32[]{:S(2)}) copy-start(bf16[512,16,128]{2,1,0:T(8,128)(2,1)} %param.8) | copy-start | bytes 6291460
  8.0 284.1 %all-reduce.2.cloned.1.call-start = ((), (), s32[]{:S(2)}) async-start(), calls=%async_computation.1 | async-start | bytes 589824 | tf_op jit(solution)/shard_map/psum | solution.py:191
  8.9 13.8 %copy-start.67 = (f32[128]{0:T(128)}, f32[128]{0:T(128)S(1)}, u32[]{:S(2)}) copy-start(f32[128]{0:T(128)S(1)} %get-tuple-element.73) | copy-start | bytes 1540
  8.9 14.6 %collective-permute-start = (s32[128]{0:T(128)S(1)}, s32[128]{0:T(128)S(1)}, u32[]{:S(2)}, u32[]{:S(2)}) collective-permute-start(s32[128]{0:T(128)S(1)} %get-tuple-element.72), channel_id=1, source_target_pairs={{0,4},{4,8},{8,12},{12,16},{16,20},{20,24},{24,28},{28,32},{32,36}... | collective-permute-start | bytes 1544 | tf_op jit(solution)/shard_map/ppermute | solution.py:20
  12.7 5.3 copy-start.69
  14.3 44.6 %copy-start.27 = (bf16[128,512]{0,1:T(8,128)(2,1)}, bf16[128,512]{0,1:T(8,128)(2,1)S(1)}, u32[]{:S(2)}) copy-start(bf16[128,512]{0,1:T(8,128)(2,1)S(1)} %slice.127) | copy-start | bytes 393220
  14.5 8.2 %copy-start.57 = (f32[128,32]{0,1:T(8,128)}, f32[128,32]{0,1:T(8,128)S(1)}, u32[]{:S(2)}) copy-start(f32[128,32]{0,1:T(8,128)S(1)} %get-tuple-element.69) | copy-start | bytes 49156
  14.5 44.4 %copy-start.65 = (bf16[128,32]{0,1:T(8,128)(2,1)}, bf16[128,32]{0,1:T(8,128)(2,1)S(1)}, u32[]{:S(2)}) copy-start(bf16[128,32]{0,1:T(8,128)(2,1)S(1)} %get-tuple-element.71) | copy-start | bytes 24580
  14.5 45.8 %collective-permute-start.1 = (bf16[128,576]{0,1:T(8,128)(2,1)S(1)}, bf16[128,576]{0,1:T(8,128)(2,1)S(1)}, u32[]{:S(2)}, u32[]{:S(2)}) collective-permute-start(bf16[128,576]{0,1:T(8,128)(2,1)S(1)} %pad_maximum_fusion.2), channel_id=1, source_target_pairs={{0,4},{4,8},{8,12},{12,16},{16,20},{20,24},{24,28},{28,32},{32,36}... | collective-permute-start | bytes 442376 | tf_op jit(solution)/shard_map/ppermute | solution.py:20
  23.5 5.4 collective-permute-start.2
  27.3 31.6 %copy-start.59 = (bf16[128,16,32]{0,2,1:T(8,128)(2,1)S(1)}, bf16[128,16,32]{0,2,1:T(8,128)(2,1)}, u32[]{:S(2)}) copy-start(bf16[128,16,32]{0,2,1:T(8,128)(2,1)} %get-tuple-element.34) | copy-start | bytes 393220
  27.3 31.6 %copy-start.62 = (bf16[128,16,32]{0,2,1:T(8,128)(2,1)S(1)}, bf16[128,16,32]{0,2,1:T(8,128)(2,1)}, u32[]{:S(2)}) copy-start(bf16[128,16,32]{0,2,1:T(8,128)(2,1)} %get-tuple-element.35) | copy-start | bytes 393220
  28.9 6.0 %collective-permute-start.4 = (s32[128]{0:T(128)S(1)}, s32[128]{0:T(128)S(1)}, u32[]{:S(2)}, u32[]{:S(2)}) collective-permute-start(s32[128]{0:T(128)S(1)} %collective-permute-done.2), channel_id=1, source_target_pairs={{0,4},{4,8},{8,12},{12,16},{16,20},{20,24},{24,28},{28,32},{32,36}... | collective-permute-start | bytes 1544 | tf_op jit(solution)/shard_map/ppermute | solution.py:20
  34.9 6.3 %collective-permute-start.6 = (s32[128]{0:T(128)S(1)}, s32[128]{0:T(128)S(1)}, u32[]{:S(2)}, u32[]{:S(2)}) collective-permute-start(s32[128]{0:T(128)S(1)} %collective-permute-done.4), channel_id=1, source_target_pairs={{0,4},{4,8},{8,12},{12,16},{16,20},{20,24},{24,28},{28,32},{32,36}... | collective-permute-start | bytes 1544 | tf_op jit(solution)/shard_map/ppermute | solution.py:20
  41.2 6.8 %collective-permute-start.8 = (s32[128]{0:T(128)S(1)}, s32[128]{0:T(128)S(1)}, u32[]{:S(2)}, u32[]{:S(2)}) collective-permute-start(s32[128]{0:T(128)S(1)} %collective-permute-done.6), channel_id=1, source_target_pairs={{0,4},{4,8},{8,12},{12,16},{16,20},{20,24},{24,28},{28,32},{32,36}... | collective-permute-start | bytes 1544 | tf_op jit(solution)/shard_map/ppermute | solution.py:20
  48.0 59.7 %copy-start.10 = (bf16[128,16,512]{0,2,1:T(8,128)(2,1)}, bf16[128,16,512]{0,2,1:T(8,128)(2,1)S(1)}, u32[]{:S(2)}) copy-start(bf16[128,16,512]{0,2,1:T(8,128)(2,1)S(1)} %slice.131) | copy-start | bytes 6291460
  48.1 5.8 %collective-permute-start.10 = (s32[128]{0:T(128)S(1)}, s32[128]{0:T(128)S(1)}, u32[]{:S(2)}, u32[]{:S(2)}) collective-permute-start(s32[128]{0:T(128)S(1)} %collective-permute-done.8), channel_id=1, source_target_pairs={{0,4},{4,8},{8,12},{12,16},{16,20},{20,24},{24,28},{28,32},{32,36}... | collective-permute-start | bytes 1544 | tf_op jit(solution)/shard_map/ppermute | solution.py:20
  53.9 6.3 %collective-permute-start.12 = (s32[128]{0:T(128)S(1)}, s32[128]{0:T(128)S(1)}, u32[]{:S(2)}, u32[]{:S(2)}) collective-permute-start(s32[128]{0:T(128)S(1)} %collective-permute-done.10), channel_id=1, source_target_pairs={{0,4},{4,8},{8,12},{12,16},{16,20},{20,24},{24,28},{28,32},{32,36}... | collective-permute-start | bytes 1544 | tf_op jit(solution)/shard_map/ppermute | solution.py:20
  58.9 6.5 %copy-start.1 = (bf16[16,128,512]{2,1,0:T(8,128)(2,1)S(1)}, bf16[16,128,512]{2,1,0:T(8,128)(2,1)}, u32[]{:S(2)}) copy-start(bf16[16,128,512]{2,1,0:T(8,128)(2,1)} %convolution_convert_fusion) | copy-start | bytes 6291460
  60.4 6.5 %copy-start.33 = (bf16[128,576]{0,1:T(8,128)(2,1)}, bf16[128,576]{0,1:T(8,128)(2,1)S(1)}, u32[]{:S(2)}) copy-start(bf16[128,576]{0,1:T(8,128)(2,1)S(1)} %collective-permute-done.1) | copy-start | bytes 442372
  60.4 7.7 %collective-permute-start.3 = (bf16[128,576]{0,1:T(8,128)(2,1)S(1)}, bf16[128,576]{0,1:T(8,128)(2,1)S(1)}, u32[]{:S(2)}, u32[]{:S(2)}) collective-permute-start(bf16[128,576]{0,1:T(8,128)(2,1)S(1)} %collective-permute-done.1), channel_id=1, source_target_pairs={{0,4},{4,8},{8,12},{12,16},{16,20},{20,24},{24,28},{28,32},{32,36}... | collective-permute-start | bytes 442376 | tf_op jit(solution)/shard_map/ppermute | solution.py:20
  68.1 6.7 %copy-start.36 = (bf16[128,576]{0,1:T(8,128)(2,1)}, bf16[128,576]{0,1:T(8,128)(2,1)S(1)}, u32[]{:S(2)}) copy-start(bf16[128,576]{0,1:T(8,128)(2,1)S(1)} %collective-permute-done.3) | copy-start | bytes 442372
  68.1 7.9 %collective-permute-start.5 = (bf16[128,576]{0,1:T(8,128)(2,1)S(1)}, bf16[128,576]{0,1:T(8,128)(2,1)S(1)}, u32[]{:S(2)}, u32[]{:S(2)}) collective-permute-start(bf16[128,576]{0,1:T(8,128)(2,1)S(1)} %collective-permute-done.3), channel_id=1, source_target_pairs={{0,4},{4,8},{8,12},{12,16},{16,20},{20,24},{24,28},{28,32},{32,36}... | collective-permute-start | bytes 442376 | tf_op jit(solution)/shard_map/ppermute | solution.py:20
  76.0 6.7 %copy-start.39 = (bf16[128,576]{0,1:T(8,128)(2,1)}, bf16[128,576]{0,1:T(8,128)(2,1)S(1)}, u32[]{:S(2)}) copy-start(bf16[128,576]{0,1:T(8,128)(2,1)S(1)} %collective-permute-done.5) | copy-start | bytes 442372
  76.0 7.9 %collective-permute-start.7 = (bf16[128,576]{0,1:T(8,128)(2,1)S(1)}, bf16[128,576]{0,1:T(8,128)(2,1)S(1)}, u32[]{:S(2)}, u32[]{:S(2)}) collective-permute-start(bf16[128,576]{0,1:T(8,128)(2,1)S(1)} %collective-permute-done.5), channel_id=1, source_target_pairs={{0,4},{4,8},{8,12},{12,16},{16,20},{20,24},{24,28},{28,32},{32,36}... | collective-permute-start | bytes 442376 | tf_op jit(solution)/shard_map/ppermute | solution.py:20
  83.9 6.7 %copy-start.42 = (bf16[128,576]{0,1:T(8,128)(2,1)}, bf16[128,576]{0,1:T(8,128)(2,1)S(1)}, u32[]{:S(2)}) copy-start(bf16[128,576]{0,1:T(8,128)(2,1)S(1)} %collective-permute-done.7) | copy-start | bytes 442372
  83.9 7.9 %collective-permute-start.9 = (bf16[128,576]{0,1:T(8,128)(2,1)S(1)}, bf16[128,576]{0,1:T(8,128)(2,1)S(1)}, u32[]{:S(2)}, u32[]{:S(2)}) collective-permute-start(bf16[128,576]{0,1:T(8,128)(2,1)S(1)} %collective-permute-done.7), channel_id=1, source_target_pairs={{0,4},{4,8},{8,12},{12,16},{16,20},{20,24},{24,28},{28,32},{32,36}... | collective-permute-start | bytes 442376 | tf_op jit(solution)/shard_map/ppermute | solution.py:20
  91.9 6.7 %copy-start.45 = (bf16[128,576]{0,1:T(8,128)(2,1)}, bf16[128,576]{0,1:T(8,128)(2,1)S(1)}, u32[]{:S(2)}) copy-start(bf16[128,576]{0,1:T(8,128)(2,1)S(1)} %collective-permute-done.9) | copy-start | bytes 442372
  91.9 7.9 %collective-permute-start.11 = (bf16[128,576]{0,1:T(8,128)(2,1)S(1)}, bf16[128,576]{0,1:T(8,128)(2,1)S(1)}, u32[]{:S(2)}, u32[]{:S(2)}) collective-permute-start(bf16[128,576]{0,1:T(8,128)(2,1)S(1)} %collective-permute-done.9), channel_id=1, source_target_pairs={{0,4},{4,8},{8,12},{12,16},{16,20},{20,24},{24,28},{28,32},{32,36}... | collective-permute-start | bytes 442376 | tf_op jit(solution)/shard_map/ppermute | solution.py:20
  99.8 7.2 %copy-start.48 = (bf16[128,576]{0,1:T(8,128)(2,1)}, bf16[128,576]{0,1:T(8,128)(2,1)S(1)}, u32[]{:S(2)}) copy-start(bf16[128,576]{0,1:T(8,128)(2,1)S(1)} %collective-permute-done.11) | copy-start | bytes 442372
  99.8 7.9 %collective-permute-start.13 = (bf16[128,576]{0,1:T(8,128)(2,1)S(1)}, bf16[128,576]{0,1:T(8,128)(2,1)S(1)}, u32[]{:S(2)}, u32[]{:S(2)}) collective-permute-start(bf16[128,576]{0,1:T(8,128)(2,1)S(1)} %collective-permute-done.11), channel_id=1, source_target_pairs={{0,4},{4,8},{8,12},{12,16},{16,20},{20,24},{24,28},{28,32},{32,36}... | collective-permute-start | bytes 442376 | tf_op jit(solution)/shard_map/ppermute | solution.py:20
  114.7 10.7 %copy-start.2 = (bf16[16,128,128]{1,2,0:T(8,128)(2,1)}, bf16[16,128,128]{1,2,0:T(8,128)(2,1)S(1)}, u32[]{:S(2)}) copy-start(bf16[16,128,128]{1,2,0:T(8,128)(2,1)S(1)} %get-tuple-element.49) | copy-start | bytes 1572868
  114.7 13.1 %copy-start.4 = (bf16[16,128,128]{1,2,0:T(8,128)(2,1)}, bf16[16,128,128]{1,2,0:T(8,128)(2,1)S(1)}, u32[]{:S(2)}) copy-start(bf16[16,128,128]{1,2,0:T(8,128)(2,1)S(1)} %get-tuple-element.53) | copy-start | bytes 1572868
  114.7 15.5 %copy-start.6 = (bf16[16,128,128]{1,2,0:T(8,128)(2,1)}, bf16[16,128,128]{1,2,0:T(8,128)(2,1)S(1)}, u32[]{:S(2)}) copy-start(bf16[16,128,128]{1,2,0:T(8,128)(2,1)S(1)} %get-tuple-element.57) | copy-start | bytes 1572868
  114.8 4.6 copy-start.11
  114.8 4.6 copy-start.60
  114.8 4.6 copy-start.63
  119.4 5.3 copy-start.23
  119.4 7.7 %copy-start.20 = (bf16[16,128,128]{1,2,0:T(8,128)(2,1)}, bf16[16,128,128]{1,2,0:T(8,128)(2,1)S(1)}, u32[]{:S(2)}) copy-start(bf16[16,128,128]{1,2,0:T(8,128)(2,1)S(1)} %get-tuple-element.43) | copy-start | bytes 1572868
  119.4 10.1 %copy-start.16 = (bf16[16,128,128]{1,2,0:T(8,128)(2,1)}, bf16[16,128,128]{1,2,0:T(8,128)(2,1)S(1)}, u32[]{:S(2)}) copy-start(bf16[16,128,128]{1,2,0:T(8,128)(2,1)S(1)} %get-tuple-element.45) | copy-start | bytes 1572868
  119.4 12.5 %copy-start.14 = (bf16[16,128,128]{1,2,0:T(8,128)(2,1)}, bf16[16,128,128]{1,2,0:T(8,128)(2,1)S(1)}, u32[]{:S(2)}) copy-start(bf16[16,128,128]{1,2,0:T(8,128)(2,1)S(1)} %get-tuple-element.46) | copy-start | bytes 1572868
  122.6 35.1 %collective-permute-start.14 = (bf16[128,576]{0,1:T(8,128)(2,1)}, bf16[128,576]{0,1:T(8,128)(2,1)}, u32[]{:S(2)}, u32[]{:S(2)}) collective-permute-start(bf16[128,576]{0,1:T(8,128)(2,1)} %pad_maximum_fusion.3), channel_id=1, source_target_pairs={{4,0},{8,4},{12,8},{16,12},{20,16},{24,20},{28,24},{32,28},{36,32}... | collective-permute-start | bytes 442376 | tf_op jit(solution)/shard_map/ppermute | solution.py:20
  155.7 4.9 copy-start.12
  155.7 4.9 copy-start.18
  155.7 4.9 copy-start.61
  155.7 4.9 copy-start.64
  158.6 8.4 %collective-permute-start.15 = (bf16[128,576]{0,1:T(8,128)(2,1)S(1)}, bf16[128,576]{0,1:T(8,128)(2,1)S(1)}, u32[]{:S(2)}, u32[]{:S(2)}) collective-permute-start(bf16[128,576]{0,1:T(8,128)(2,1)S(1)} %fusion.53), channel_id=1, source_target_pairs={{4,0},{8,4},{12,8},{16,12},{20,16},{24,20},{28,24},{32,28},{36,32}... | collective-permute-start | bytes 442376 | tf_op jit(solution)/shard_map/ppermute | solution.py:20
  160.6 6.4 %copy-start.53 = (f32[128,512]{0,1:T(8,128)S(1)}, f32[128,512]{0,1:T(8,128)}, u32[]{:S(2)}) copy-start(f32[128,512]{0,1:T(8,128)} %fusion.20) | copy-start | bytes 786436
  160.6 6.4 %slice-start.2 = ((f32[128,576]{0,1:T(8,128)}), f32[128,64]{0,1:T(8,128)S(1)}, s32[]{:S(2)}) async-start(f32[128,576]{0,1:T(8,128)} %copy-done.56), calls=%async_computation.5 | async-start | bytes 65536 | tf_op jit(solution)/shard_map/slice | solution.py:171
  161.4 16.1 %copy-start.22 = (bf16[16,128,128]{1,2,0:T(8,128)(2,1)S(1)}, bf16[16,128,128]{1,2,0:T(8,128)(2,1)}, u32[]{:S(2)}) copy-start(bf16[16,128,128]{1,2,0:T(8,128)(2,1)} %get-tuple-element.42) | copy-start | bytes 1572868
  167.1 8.2 %collective-permute-start.16 = (bf16[128,576]{0,1:T(8,128)(2,1)S(1)}, bf16[128,576]{0,1:T(8,128)(2,1)S(1)}, u32[]{:S(2)}, u32[]{:S(2)}) collective-permute-start(bf16[128,576]{0,1:T(8,128)(2,1)S(1)} %fusion.54), channel_id=1, source_target_pairs={{4,0},{8,4},{12,8},{16,12},{20,16},{24,20},{28,24},{32,28},{36,32}... | collective-permute-start | bytes 442376 | tf_op jit(solution)/shard_map/ppermute | solution.py:20
  175.3 9.6 %collective-permute-start.17 = (bf16[128,576]{0,1:T(8,128)(2,1)S(1)}, bf16[128,576]{0,1:T(8,128)(2,1)S(1)}, u32[]{:S(2)}, u32[]{:S(2)}) collective-permute-start(bf16[128,576]{0,1:T(8,128)(2,1)S(1)} %fusion.55), channel_id=1, source_target_pairs={{4,0},{8,4},{12,8},{16,12},{20,16},{24,20},{28,24},{32,28},{36,32}... | collective-permute-start | bytes 442376 | tf_op jit(solution)/shard_map/ppermute | solution.py:20
  177.5 7.5 %copy-start.52 = (f32[128,512]{0,1:T(8,128)S(1)}, f32[128,512]{0,1:T(8,128)}, u32[]{:S(2)}) copy-start(f32[128,512]{0,1:T(8,128)} %fusion.22) | copy-start | bytes 786436
  177.5 7.5 %slice-start.1 = ((f32[128,576]{0,1:T(8,128)}), f32[128,64]{0,1:T(8,128)S(1)}, s32[]{:S(2)}) async-start(f32[128,576]{0,1:T(8,128)} %copy-done.55), calls=%async_computation.4 | async-start | bytes 65536 | tf_op jit(solution)/shard_map/slice | solution.py:171
  178.3 19.3 %copy-start.25 = (bf16[16,128,128]{1,2,0:T(8,128)(2,1)S(1)}, bf16[16,128,128]{1,2,0:T(8,128)(2,1)}, u32[]{:S(2)}) copy-start(bf16[16,128,128]{1,2,0:T(8,128)(2,1)} %get-tuple-element.47) | copy-start | bytes 1572868
  185.0 10.6 %collective-permute-start.18 = (bf16[128,576]{0,1:T(8,128)(2,1)S(1)}, bf16[128,576]{0,1:T(8,128)(2,1)S(1)}, u32[]{:S(2)}, u32[]{:S(2)}) collective-permute-start(bf16[128,576]{0,1:T(8,128)(2,1)S(1)} %fusion.56), channel_id=1, source_target_pairs={{4,0},{8,4},{12,8},{16,12},{20,16},{24,20},{28,24},{32,28},{36,32}... | collective-permute-start | bytes 442376 | tf_op jit(solution)/shard_map/ppermute | solution.py:20
  195.6 10.2 %collective-permute-start.19 = (bf16[128,576]{0,1:T(8,128)(2,1)S(1)}, bf16[128,576]{0,1:T(8,128)(2,1)S(1)}, u32[]{:S(2)}, u32[]{:S(2)}) collective-permute-start(bf16[128,576]{0,1:T(8,128)(2,1)S(1)} %fusion.57), channel_id=1, source_target_pairs={{4,0},{8,4},{12,8},{16,12},{20,16},{24,20},{28,24},{32,28},{36,32}... | collective-permute-start | bytes 442376 | tf_op jit(solution)/shard_map/ppermute | solution.py:20
  197.6 8.3 %copy-start.51 = (f32[128,512]{0,1:T(8,128)S(1)}, f32[128,512]{0,1:T(8,128)}, u32[]{:S(2)}) copy-start(f32[128,512]{0,1:T(8,128)} %fusion.24) | copy-start | bytes 786436
  197.6 8.3 %slice-start = ((f32[128,576]{0,1:T(8,128)}), f32[128,64]{0,1:T(8,128)S(1)}, s32[]{:S(2)}) async-start(f32[128,576]{0,1:T(8,128)} %copy-done.54), calls=%async_computation.3 | async-start | bytes 65536 | tf_op jit(solution)/shard_map/slice | solution.py:171
  198.4 18.9 %copy-start.13 = (bf16[128,16,128]{2,1,0:T(8,128)(2,1)S(1)}, bf16[128,16,128]{2,1,0:T(8,128)(2,1)}, u32[]{:S(2)}) copy-start(bf16[128,16,128]{2,1,0:T(8,128)(2,1)} %param.9) | copy-start | bytes 1572868
  205.9 10.5 %collective-permute-start.20 = (bf16[128,576]{0,1:T(8,128)(2,1)S(1)}, bf16[128,576]{0,1:T(8,128)(2,1)S(1)}, u32[]{:S(2)}, u32[]{:S(2)}) collective-permute-start(bf16[128,576]{0,1:T(8,128)(2,1)S(1)} %fusion.58), channel_id=1, source_target_pairs={{4,0},{8,4},{12,8},{16,12},{20,16},{24,20},{28,24},{32,28},{36,32}... | collective-permute-start | bytes 442376 | tf_op jit(solution)/shard_map/ppermute | solution.py:20
  217.2 350.7 %reduce-scatter.2.cloned.1.call-start = ((), (), s32[]{:S(2)}) async-start(), calls=%async_computation.2 | async-start | bytes 4259840 | tf_op jit(solution)/shard_map/reduce_scatter | solution.py:202
  255.2 37.9 %copy-start.68 = (f32[128]{0:T(128)S(1)}, f32[128]{0:T(128)}, u32[]{:S(2)}) copy-start(f32[128]{0:T(128)} %copy-done.67) | copy-start | bytes 1540
  255.2 37.9 %copy-start.70 = (f32[32]{0:T(128)S(1)}, f32[32]{0:T(128)}, u32[]{:S(2)}) copy-start(f32[32]{0:T(128)} %copy-done.69) | copy-start | bytes 388
  (34 other events, 78.4 us)
Sparse Core Ops, SparseCore 0:
  217.3 74.7 all-reduce.1
Sparse Core Ops, SparseCore 1:
  221.8 346.1 reduce-scatter.1
where the time goes:
time: 589 us; the launch traced here: 577 us
  waiting for transfers between devices  362 us (61%)
  matrix products  89.6 us (15%)
  starting transfers between devices  81 us (14%)
  other arithmetic  17.5 us (3%)
  between operations  17 us (3%)
  local copies, waits for them, and re-layouts  10.4 us (2%)
    reduce_scatter x1, waiting for transfers between devices, body(): lax.psum_scatter(jnp.einsum('hqc,qhv->chv', o_lat, cotangent, preferred_e...  273 us
    ppermute x21, starting transfers between devices, shifted(): return lax.ppermute(value, axis, pairs)  81 us
    ppermute x21, waiting for transfers between devices, shifted(): return lax.ppermute(value, axis, pairs)  52.9 us
    psum x1, waiting for transfers between devices, body(): summed = lax.psum(returned + key_grads[0], 'head')  35.3 us
    dot_general x8, matrix products, block_grads(): jnp.einsum('hqk,kd->qhd', d_scores, k_block, preferred_element_type=jnp.f...  25 us
    dot_general x8, matrix products, value_sum(): jnp.einsum('hqk,kc->hqc', prob_tile, k_block[:, :D_C], preferred_element_...  22.5 us
  transfers between devices with their start and end apart: 23, of which 19 were waited for; matrix products, arithmetic and copies ran while one was open for 17% of the time, Pallas kernels for 0%

commit v1 on v0

v1 whole, which is shorter than its diff:
```python
import math

import jax
import jax.numpy as jnp
import numpy as np
from jax import lax
from jax.experimental import pallas as pl
from jax.experimental.pallas import tpu as pltpu
from jax.sharding import PartitionSpec as P

F32, BF16 = jnp.float32, jnp.bfloat16
MESH = pl.DeviceIdType.MESH
SCALE = 1.0 / math.sqrt(192.0)
LOG2E = 1.4426950408889634
FREQUENCY = [
    float(f) for f in np.asarray(10000.0 ** (-2.0 * np.arange(32, dtype=np.float32) / 64), np.float32)
]


def dot(a, b):
    return jnp.dot(a, b, preferred_element_type=F32)


def dot_nt(a, b):
    return lax.dot_general(a, b, (((1,), (1,)), ((), ())), preferred_element_type=F32)


def swap_halves(x):
    lane = lax.broadcasted_iota(jnp.int32, x.shape, 1)
    return jnp.where(lane < 32, pltpu.roll(x, 96, 1), pltpu.roll(x, 32, 1))


def widened(x):
    return jnp.concatenate([x, jnp.zeros_like(x)], axis=1)


def kernel(
    q_hbm, lat_hbm, pos_ref, vup_hbm, cot_hbm,
    attn_hbm, gq_hbm, gl_hbm, gv_hbm,
    q_raw, lat_raw, vup_raw, cot_raw, tab, sbuf, dpbuf, q_hm, q_t, do_hm, do_t, vup_h, cot_h,
    p_buf, ds_buf, bias, ao, kw, k_t,
    dup_s, rx, ry, xs, rxy, ys, ryx, zs, rz, gv,
    dks, drow, zsend, zrecv, glt, gl,
    in_sem, out_sem, kz_s, kz_r, kr_s, kr_r,
    rx_s, rx_r, ry_s, ry_r, rxy_s, rxy_r, ryx_s, ryx_r, rz_s, rz_r,
    dr_s, dr_r, dz_s, dz_r, gl_s, gl_r,
):
    ctx, head = lax.axis_index("ctx"), lax.axis_index("head")
    a, row = ctx % 2, ctx // 2
    y, z = ctx // 16, (ctx // 2) % 8
    me = a * 4 + head
    partner = ctx + 1 - 2 * a

    def mate(t):
        m = (me + t) % 8
        return m, m // 4, m % 4

    def rcopy(src, dst, ss, rs, to_ctx, to_head):
        return pltpu.make_async_remote_copy(
            src_ref=src, dst_ref=dst, send_sem=ss, recv_sem=rs,
            device_id=(to_ctx, to_head), device_id_type=MESH,
        )

    in_copies = [
        pltpu.make_async_copy(src, dst, in_sem.at[i])
        for i, (src, dst) in enumerate(
            ((lat_hbm, lat_raw), (vup_hbm, vup_raw), (cot_hbm, cot_raw), (q_hbm, q_raw))
        )
    ]
    for c in in_copies:
        c.start()

    partners = []
    for t in range(1, 8):
        m, a2, h2 = mate(t)
        partners.append((row * 2 + a2, h2))
    for d in (1, 2, 3, 4):
        partners.append(((ctx + 2 * d) % 64, head))
        partners.append(((ctx + 64 - 2 * d) % 64, head))
    partners.append(((ctx + 64 - 7 + 14 * a) % 64, head))
    for t in range(1, 4):
        partners.append((((y + t) % 4) * 16 + ctx % 16, head))
    for t in range(1, 8):
        partners.append((y * 16 + ((z + t) % 8) * 2 + a, head))
    barrier = pltpu.get_barrier_semaphore()
    for c, h in partners:
        pl.semaphore_signal(barrier, inc=1, device_id=(c, h), device_id_type=MESH)

    lane = lax.broadcasted_iota(jnp.int32, (128, 128), 1)
    freq_row = jnp.zeros((8, 128), F32)
    lane8 = lax.broadcasted_iota(jnp.int32, (8, 128), 1) % 32
    for i in range(32):
        freq_row = jnp.where(lane8 == i, FREQUENCY[i], freq_row)
    pos_col = jnp.broadcast_to(pos_ref[...].astype(F32), (128, 128)).T
    angle = pos_col * freq_row[:1]
    sine = jnp.where(lane < 32, -jnp.sin(angle), jnp.sin(angle))
    tab[0] = jnp.where(lane < 64, jnp.cos(angle), 0.0)
    tab[1] = jnp.where(lane < 64, sine, 0.0)

    in_copies[0].wait()
    own = 7 * 128
    kw[own:own + 128, :512] = lat_raw[:, :512]
    k_rope = widened(lat_raw[:, 512:].astype(F32))
    k_rope = k_rope * tab[0] + swap_halves(k_rope) * tab[1]
    kw[own:own + 128, 512:] = k_rope[:, :64].astype(BF16)

    pl.semaphore_wait(barrier, len(partners))

    def krows(slot, h):
        return kw.at[pl.ds(pl.multiple_of(slot * 128 + h * 32, 32), 32)]

    def kz(d):
        to = (ctx + (2 * d if d < 4 else 7)) % 64
        return rcopy(krows(7, head), krows(7 - 2 * d if d < 4 else 0, head), kz_s.at[d], kz_r.at[d], to, head)

    def kfwd(d, t):
        m, a2, h2 = mate(t)
        return rcopy(
            krows(7 - 2 * d, head), krows(7 - (2 * d + a2 - a), head),
            kr_s.at[d, t], kr_r.at[d, me], row * 2 + a2, h2,
        )

    def kgot(d, t):
        m, a2, h2 = mate(t)
        ref = krows(7 - (2 * d + a - a2), h2)
        return rcopy(ref, ref, kr_s.at[d, t], kr_r.at[d, m], row * 2 + a2, h2)

    def kfirst(h2):
        return rcopy(krows(7, head), krows(6, head), kr_s.at[0, h2], kr_r.at[0, head], row * 2 + 1, h2)

    def kfirst_got(h2):
        return rcopy(krows(6, h2), krows(6, h2), kr_s.at[0, h2], kr_r.at[0, h2], row * 2, h2)

    def klast(t):
        return rcopy(krows(0, head), krows(0, head), kr_s.at[4, t], kr_r.at[4, head], row * 2, (head + t) % 4)

    def klast_got(t):
        h2 = (head + t) % 4
        return rcopy(krows(0, h2), krows(0, h2), kr_s.at[4, t], kr_r.at[4, h2], row * 2, h2)

    for d in (1, 2, 3):
        kz(d).start()

    @pl.when(a == 1)
    def _():
        kz(4).start()

    @pl.when(a == 0)
    def _():
        for h2 in range(4):
            kfirst(h2).start()

    def forward(d):
        kz(d).wait_recv()
        for t in range(1, 8):
            kfwd(d, t).start()

    def vup_in(i, c):
        v = vup_raw[pl.ds(i * 8, 8)].astype(F32).reshape(128, 128)
        sbuf[i // 16, pl.ds((i % 16) * 128, 128), :] = v
        return c

    def cot_in(i, c):
        sbuf[4, pl.ds(i * 128, 128), :] = cot_raw[pl.ds(i * 8, 8)].astype(F32).reshape(128, 128)
        return c

    def q_in(i, c):
        for j in range(5):
            w = 128 if j < 4 else 64
            x = q_raw[pl.ds(i * 8, 8), :, j * 128:j * 128 + w].astype(F32).reshape(128, w)
            dpbuf[j, pl.ds(i * 128, 128), :] = x if w == 128 else widened(x)
        return c

    def head_up(h, c):
        rows = pl.ds(h * 128, 128)
        for cc in range(4):
            vup_h[h, cc * 128:(cc + 1) * 128, :] = sbuf[cc, pl.ds(h, 128, stride=16), :].astype(BF16)
        cot = sbuf[4, pl.ds(h, 128, stride=16), :].astype(BF16)
        cot_h[h] = cot
        v = vup_h[h]
        do_hm[rows, :] = dot_nt(cot, v).astype(BF16)
        do_t[:, rows] = dot_nt(v, cot).astype(BF16)
        return c

    def head_q(h, c):
        rows = pl.ds(h * 128, 128)
        for j in range(4):
            x = dpbuf[j, pl.ds(h, 128, stride=16), :].astype(BF16)
            q_hm[rows, j * 128:(j + 1) * 128] = x
            q_t[j * 128:(j + 1) * 128, rows] = x.T
        x = dpbuf[4, pl.ds(h, 128, stride=16), :]
        x = (x * tab[0] + swap_halves(x) * tab[1]).astype(BF16)
        q_hm[rows, 512:576] = x[:, :64]
        q_t[512:576, rows] = x.T[:64]
        return c

    in_copies[1].wait()
    lax.fori_loop(0, 64, vup_in, 0)
    in_copies[2].wait()
    lax.fori_loop(0, 16, cot_in, 0)
    forward(1)
    lax.fori_loop(0, 16, head_up, 0)
    forward(2)
    in_copies[3].wait()
    lax.fori_loop(0, 16, q_in, 0)
    forward(3)
    lax.fori_loop(0, 16, head_q, 0)

    @pl.when(a == 0)
    def _():
        kz(4).wait_recv()
        for t in range(1, 4):
            klast(t).start()

    q_idx = lax.broadcasted_iota(jnp.int32, (128, 128), 0)
    pos_row = pos_col.astype(jnp.int32)
    for w in range(8):
        back = 896 - w * 128 + q_idx - lane
        bias[:, w * 128:(w + 1) * 128] = jnp.where((back >= 0) & (back <= pos_row), 0.0, -jnp.inf)

    def score_group(g):
        cols = slice(g * 256, g * 256 + 256)
        for w in (2 * g, 2 * g + 1):
            k_t[:, w * 128:(w + 1) * 128] = kw[w * 128:(w + 1) * 128, :].T

        def qk(r, c):
            rows = pl.ds(r * 512, 512)
            s = dot(q_hm[rows, :], k_t[:, cols])
            sbuf[2 * g, rows, :] = s[:, :128]
            sbuf[2 * g + 1, rows, :] = s[:, 128:]
            s = dot(do_hm[rows, :], k_t[:512, cols])
            dpbuf[2 * g, rows, :] = s[:, :128]
            dpbuf[2 * g + 1, rows, :] = s[:, 128:]
            return c

        lax.fori_loop(0, 4, qk, 0)

    def arrived(d):
        for t in range(1, 8):
            kgot(d, t).wait_recv()

    @pl.when(a == 1)
    def _():
        for h2 in range(4):
            kfirst_got(h2).wait_recv()

    arrived(1)
    score_group(3)
    arrived(2)
    score_group(2)
    arrived(3)
    score_group(1)

    @pl.when(a == 0)
    def _():
        for t in range(1, 4):
            klast_got(t).wait_recv()

    score_group(0)

    def x_copy(hg):
        return rcopy(dup_s.at[pl.ds(4 * hg, 2), 1 - a], rx.at[hg], rx_s.at[hg], rx_r.at[hg], partner, head)

    def y_to(t):
        return ((y + t) % 4) * 16 + ctx % 16

    def y_copy(hg, t):
        y2 = (y + t) % 4
        return rcopy(
            dup_s.at[pl.ds(4 * hg + 2, 2), :, pl.ds(pl.multiple_of(64 * y2, 64), 64)], ry.at[hg, t - 1],
            ry_s.at[hg, t - 1], ry_r.at[hg, t - 1], y_to(t), head,
        )

    def xy_copy(hg, t):
        y2 = (y + t) % 4
        return rcopy(
            xs.at[hg, :, pl.ds(pl.multiple_of(64 * y2, 64), 64)], rxy.at[hg, t - 1],
            rxy_s.at[hg, t - 1], rxy_r.at[hg, t - 1], y_to(t), head,
        )

    def yx_copy(hg):
        return rcopy(ys.at[hg, :, 1 - a], ryx.at[hg], ryx_s.at[hg], ryx_r.at[hg], partner, head)

    def z_copy(hg, t):
        z2 = (z + t) % 8
        rows = pl.ds(pl.multiple_of(32 * hg, 32), 32)
        return rcopy(
            zs.at[z2, rows], rz.at[t - 1, rows], rz_s.at[hg, t - 1], rz_r.at[hg, t - 1],
            y * 16 + z2 * 2 + a, head,
        )

    own_y = pl.ds(pl.multiple_of(64 * y, 64), 64)

    def up_second(hg):
        x_copy(hg).wait_recv()
        for j in range(2):
            xs[hg, j] = dup_s[4 * hg + j, a].astype(F32) + rx[hg, j].astype(F32)
        for t in range(1, 4):
            xy_copy(hg, t).start()
        for t in range(1, 4):
            y_copy(hg, t).wait_recv()
        for j in range(2):
            for half in range(2):
                total = dup_s[4 * hg + 2 + j, half, own_y, :].astype(F32)
                for t in range(3):
                    total = total + ry[hg, t, j, half].astype(F32)
                ys[hg, j, half] = total
        yx_copy(hg).start()

    def up_third(hg):
        for t in range(1, 4):
            xy_copy(hg, t).wait_recv()
        yx_copy(hg).wait_recv()
        for j in range(2):
            total = xs[hg, j, own_y, :]
            for t in range(3):
                total = total + rxy[hg, t, j]
            zs[:, pl.ds(pl.multiple_of((4 * hg + j) * 8, 8), 8), :] = total.reshape(8, 8, 128)
            total = ys[hg, j, a] + ryx[hg, j]
            zs[:, pl.ds(pl.multiple_of((4 * hg + 2 + j) * 8, 8), 8), :] = total.reshape(8, 8, 128)
        for t in range(1, 8):
            z_copy(hg, t).start()

    def up_last(hg):
        for t in range(1, 8):
            z_copy(hg, t).wait_recv()
        rows = pl.ds(pl.multiple_of(32 * hg, 32), 32)
        total = zs[z, rows, :]
        for t in range(7):
            total = total + rz[t, rows, :]
        for j in range(4):
            gv[pl.ds(4 * hg + j, 8, stride=16), :] = total[8 * j:8 * j + 8]

    def group(hg, c):
        def soft(r, c2):
            q0 = pl.multiple_of((r % 4) * 32, 32)
            rows = pl.ds(pl.multiple_of(hg * 512 + r * 32, 32), 32)
            s = [sbuf[w, rows, :] + bias[pl.ds(q0, 32), w * 128:(w + 1) * 128] for w in range(8)]
            m = s[0]
            for w in range(1, 8):
                m = jnp.maximum(m, s[w])
            m = jnp.max(m, axis=1, keepdims=True)
            e = [jnp.exp2((x - m) * (SCALE * LOG2E)) for x in s]
            mass = e[0]
            for w in range(1, 8):
                mass = mass + e[w]
            inverse = 1.0 / jnp.sum(mass, axis=1, keepdims=True)
            p = [(x * inverse).astype(BF16) for x in e]
            delta = jnp.zeros((32, 128), F32)
            for w in range(8):
                p_buf[rows, w * 128:(w + 1) * 128] = p[w]
                delta = delta + p[w].astype(F32) * dpbuf[w, rows, :]
            delta = jnp.sum(delta, axis=1, keepdims=True)
            for w in range(8):
                ds = p[w].astype(F32) * (dpbuf[w, rows, :] - delta) * SCALE
                ds_buf[rows, w * 128:(w + 1) * 128] = ds.astype(BF16)
            return c2

        lax.fori_loop(0, 16, soft, 0)
        rows = pl.ds(pl.multiple_of(hg * 512, 512), 512)
        o = dot(p_buf[rows, :], kw[:, :512]).astype(BF16)
        for j in range(4):
            h = hg * 4 + j
            oh = o[j * 128:(j + 1) * 128]
            ao[pl.ds(h, 128, stride=16), :] = dot(oh, vup_h[h])
            up = dot(oh.T, cot_h[h]).reshape(32, 2, 8, 128)
            for half in range(2):
                dup_s[h, half] = up[:, half].reshape(256, 128).astype(BF16)
        x_copy(hg).start()
        for t in range(1, 4):
            y_copy(hg, t).start()

        @pl.when(hg >= 1)
        def _():
            up_second(hg - 1)

        @pl.when(hg >= 2)
        def _():
            up_third(hg - 2)

        return c

    lax.fori_loop(0, 4, group, 0)

    def quarter(slot, j):
        return dks.at[slot, pl.ds(pl.multiple_of(144 * j, 16), 144)]

    def dr_copy(d, t):
        m, a2, h2 = mate(t)
        return rcopy(
            quarter(7 - (2 * d + a - a2), h2), drow.at[d, me], dr_s.at[d, t], dr_r.at[d, me], row * 2 + a2, h2
        )

    def dr_got(d, t):
        m, a2, h2 = mate(t)
        return rcopy(drow.at[d, m], drow.at[d, m], dr_s.at[d, t], dr_r.at[d, m], row * 2 + a2, h2)

    def dr_last(h2):
        return rcopy(quarter(0, h2), drow.at[4, head], dr_s.at[4, h2], dr_r.at[4, head], row * 2 + 1, h2)

    def dr_last_got(h2):
        return rcopy(drow.at[4, h2], drow.at[4, h2], dr_s.at[4, h2], dr_r.at[4, h2], row * 2, h2)

    def dz_copy(d):
        return rcopy(zsend.at[d], zrecv.at[d], dz_s.at[d], dz_r.at[d], (ctx + 64 - 2 * d) % 64, head)

    def same_row(t):
        m, a2, h2 = mate(t)
        return a2 <= a

    def same_row_got(t):
        m, a2, h2 = mate(t)
        return a2 >= a

    def key_grads(g):
        cols = slice(g * 256, g * 256 + 256)
        x = dot(q_t[...], ds_buf[:, cols])
        v = dot(do_t[...], p_buf[:, cols])
        for i in range(2):
            part = slice(128 * i, 128 * i + 128)
            dks[2 * g + i, :512, :] = (x[:512, part] + v[:, part]).astype(BF16)
            dks[2 * g + i, 512:, :] = x[512:, part].astype(BF16)

    def row_sum(d):
        for t in range(1, 8):
            dr_got(d, t).wait_recv()
        total = quarter(7 - 2 * d, head)[...].astype(F32)
        for t in range(1, 8):
            total = total + drow[d, (me + t) % 8].astype(F32)
        zsend[d] = total.astype(BF16)
        dz_copy(d).start()

    @pl.when(a == 1)
    def _():
        drow[0, 0:4] = jnp.zeros((4, 144, 128), BF16)

    @pl.when(a == 0)
    def _():
        zrecv[4] = jnp.zeros((144, 128), BF16)

    key_grads(0)

    @pl.when(a == 0)
    def _():
        for h2 in range(4):
            dr_last(h2).start()

    up_second(3)
    up_third(2)
    key_grads(1)
    for t in range(1, 8):
        dr_copy(3, t).start()
    up_third(3)
    key_grads(2)
    for t in range(1, 8):
        dr_copy(2, t).start()
    row_sum(3)

    @pl.when(a == 1)
    def _():
        for h2 in range(4):
            dr_last_got(h2).wait_recv()
        total = drow[4, 0].astype(F32)
        for h2 in range(1, 4):
            total = total + drow[4, h2].astype(F32)
        zsend[4] = total.astype(BF16)
        dz_copy(4).start()

    key_grads(3)
    for t in range(1, 8):
        dr_copy(1, t).start()
    for t in range(1, 8):
        @pl.when(same_row(t))
        def _():
            dr_copy(0, t).start()
    row_sum(2)

    def dq(r, c):
        x = dot(ds_buf[pl.ds(pl.multiple_of(r * 512, 512), 512), :], kw[...])
        for j in range(4):
            h = r * 4 + j
            part = x[j * 128:(j + 1) * 128]
            for t in range(4):
                dpbuf[t, pl.ds(h, 128, stride=16), :] = part[:, t * 128:(t + 1) * 128]
            rope = widened(part[:, 512:])
            dpbuf[4, pl.ds(h, 128, stride=16), :] = rope * tab[0] - swap_halves(rope) * tab[1]
        return c

    lax.fori_loop(0, 2, dq, 0)
    row_sum(1)

    def last(hg, c):
        up_last(hg)
        return c

    lax.fori_loop(0, 4, last, 0)
    lax.fori_loop(2, 4, dq, 0)

    for t in range(1, 8):
        @pl.when(same_row_got(t))
        def _():
            dr_got(0, t).wait_recv()
    total = quarter(7, head)[...].astype(F32)
    for t in range(1, 8):
        total = total + drow[0, (me + t) % 8].astype(F32)
    for d in (1, 2, 3):
        dz_copy(d).wait_recv()

    @pl.when(a == 1)
    def _():
        dz_copy(4).wait_recv()

    for d in (1, 2, 3, 4):
        total = total + zrecv[d].astype(F32)
    roped = head == 3
    cosine = jnp.where(roped, tab[0].T[:32], 1.0)
    sine = jnp.where(roped, tab[1].T[32:64], 0.0)
    lower, upper = total[80:112], total[112:144]
    own_quarter = glt.at[pl.ds(pl.multiple_of(144 * head, 16), 144)]
    own_quarter[...] = jnp.concatenate(
        [total[:80], lower * cosine + upper * sine, upper * cosine - lower * sine], axis=0
    ).astype(BF16)

    def gl_copy(t):
        return rcopy(own_quarter, own_quarter, gl_s.at[t], gl_r.at[head], ctx, (head + t) % 4)

    def gl_got(t):
        h2 = (head + t) % 4
        ref = glt.at[pl.ds(pl.multiple_of(144 * h2, 16), 144)]
        return rcopy(ref, ref, gl_s.at[t], gl_r.at[h2], ctx, h2)

    for t in range(1, 4):
        gl_copy(t).start()

    def out16(i, c):
        toks = pl.ds(i * 8, 8)
        cot_raw[toks] = ao[pl.ds(i * 128, 128), :].reshape(8, 16, 128).astype(BF16)
        for j in range(5):
            w = 128 if j < 4 else 64
            part = dpbuf[j, pl.ds(i * 128, 128), :]
            q_raw[toks, :, j * 128:j * 128 + w] = part[:, :w].reshape(8, 16, w).astype(BF16)
        return c

    outs = [pltpu.make_async_copy(gv, gv_hbm, out_sem.at[0])]
    outs[0].start()
    for i in range(4):
        lax.fori_loop(4 * i, 4 * i + 4, out16, 0)
        toks = pl.ds(32 * i, 32)
        outs.append(pltpu.make_async_copy(q_raw.at[toks], gq_hbm.at[toks], out_sem.at[1 + i]))
        outs[-1].start()
    outs.append(pltpu.make_async_copy(cot_raw, attn_hbm, out_sem.at[5]))
    outs[-1].start()
    for t in range(1, 4):
        gl_got(t).wait_recv()
    gl[...] = glt[...].T
    outs.append(pltpu.make_async_copy(gl, gl_hbm, out_sem.at[6]))
    outs[-1].start()

    for d in (1, 2, 3):
        kz(d).wait_send()
        for t in range(1, 8):
            kfwd(d, t).wait_send()
            dr_copy(d, t).wait_send()
        dz_copy(d).wait_send()

    @pl.when(a == 1)
    def _():
        kz(4).wait_send()
        dz_copy(4).wait_send()

    @pl.when(a == 0)
    def _():
        for h2 in range(4):
            kfirst(h2).wait_send()
            dr_last(h2).wait_send()
        for t in range(1, 4):
            klast(t).wait_send()

    for t in range(1, 8):
        @pl.when(same_row(t))
        def _():
            dr_copy(0, t).wait_send()

    for t in range(1, 4):
        gl_copy(t).wait_send()

    def drained(hg, c):
        x_copy(hg).wait_send()
        yx_copy(hg).wait_send()
        for t in range(1, 4):
            y_copy(hg, t).wait_send()
            xy_copy(hg, t).wait_send()
        for t in range(1, 8):
            z_copy(hg, t).wait_send()
        return c

    lax.fori_loop(0, 4, drained, 0)
    for c in outs:
        c.wait()


def body(queries, latent_kv, positions, value_up, cotangent):
    anywhere = pl.BlockSpec(memory_space=pl.ANY)
    vmem, dma = pltpu.VMEM, pltpu.SemaphoreType.DMA
    attn, gq, gl, gv = pl.pallas_call(
        kernel,
        out_shape=(
            jax.ShapeDtypeStruct((128, 16, 128), BF16),
            jax.ShapeDtypeStruct((128, 16, 576), BF16),
            jax.ShapeDtypeStruct((128, 576), BF16),
            jax.ShapeDtypeStruct((128, 128), F32),
        ),
        in_specs=[anywhere, anywhere, pl.BlockSpec(memory_space=pltpu.VMEM), anywhere, anywhere],
        out_specs=(anywhere,) * 4,
        scratch_shapes=[
            vmem((128, 16, 576), BF16), vmem((128, 576), BF16), vmem((512, 16, 128), BF16),
            vmem((128, 16, 128), BF16), vmem((2, 128, 128), F32),
            vmem((8, 2048, 128), F32), vmem((8, 2048, 128), F32),
            vmem((2048, 576), BF16), vmem((576, 2048), BF16), vmem((2048, 512), BF16), vmem((512, 2048), BF16),
            vmem((16, 512, 128), BF16), vmem((16, 128, 128), BF16),
            vmem((2048, 1024), BF16), vmem((2048, 1024), BF16), vmem((128, 1024), F32), vmem((2048, 128), F32),
            vmem((1024, 576), BF16), vmem((576, 1024), BF16),
            vmem((16, 2, 256, 128), BF16), vmem((4, 2, 256, 128), BF16), vmem((4, 3, 2, 2, 64, 128), BF16),
            vmem((4, 2, 256, 128), F32), vmem((4, 3, 2, 64, 128), F32), vmem((4, 2, 2, 64, 128), F32),
            vmem((4, 2, 64, 128), F32), vmem((8, 128, 128), F32), vmem((7, 128, 128), F32), vmem((128, 128), F32),
            vmem((8, 576, 128), BF16), vmem((5, 8, 144, 128), BF16), vmem((5, 144, 128), BF16),
            vmem((5, 144, 128), BF16), vmem((576, 128), BF16), vmem((128, 576), BF16),
            dma((4,)), dma((7,)), dma((5,)), dma((5,)), dma((5, 8)), dma((5, 8)),
            dma((4,)), dma((4,)), dma((4, 3)), dma((4, 3)), dma((4, 3)), dma((4, 3)), dma((4,)), dma((4,)),
            dma((4, 7)), dma((4, 7)),
            dma((5, 8)), dma((5, 8)), dma((5,)), dma((5,)), dma((4,)), dma((4,)),
        ],
        compiler_params=pltpu.CompilerParams(
            collective_id=0, has_side_effects=True, vmem_limit_bytes=64 * 2**20 - 2**16
        ),
    )(queries, latent_kv, positions.reshape(1, 128), value_up, cotangent)
    return attn, gq, gl, gv.reshape(8, 16, 128)


def solution(mesh):
    in_specs = (
        P("ctx", "head", None),
        P("ctx", None),
        P("ctx"),
        P(None, "head", None),
        P("ctx", "head", None),
    )
    out_specs = (
        P("ctx", "head", None),
        P("ctx", "head", None),
        P("ctx", None),
        P("ctx", "head", None),
    )
    return jax.shard_map(body, mesh=mesh, in_specs=in_specs, out_specs=out_specs, check_vma=False)
```

time: 589 us -> 112 us (0.19); the launches traced: 577 us -> 110 us
  waiting for transfers between devices: 362 us -> 0 us
  Pallas kernels: 0 us -> 94.7 us
  matrix products: 89.6 us -> 0 us
  starting transfers between devices: 81 us -> 0 us
  other arithmetic: 17.5 us -> 0 us
  between operations: 17 us -> 0.64 us
    reduce_scatter x1 -> x0, waiting for transfers between devices: 273 us -> none  [body(): lax.psum_scatter(jnp.einsum('hqc,qhv->chv', o_lat, cotangent, preferred_e...]
    pallas_call x0 -> x1, Pallas kernels: none -> 94.7 us  [body(): pl.pallas_call(kernel, out_shape=(jax.ShapeDtypeStruct((128, 16, 128), BF...]
    dot_general x51 -> x0, matrix products: 89.6 us -> none  [the longest x8 25 us: block_grads(): jnp.einsum('hqk,kd->qhd', d_scores, k_block, preferred_element_type=jnp.f...]
    ppermute x21 -> x0, starting transfers between devices: 81 us -> none  [shifted(): return lax.ppermute(value, axis, pairs)]
    ppermute x21 -> x0, waiting for transfers between devices: 52.9 us -> none  [shifted(): return lax.ppermute(value, axis, pairs)]
    psum x1 -> x0, waiting for transfers between devices: 35.3 us -> none  [body(): summed = lax.psum(returned + key_grads[0], 'head')]
    unnamed x144 -> x10, local copies, waits for them, and re-layouts: 4.19 us -> 14.5 us
    convert_element_type x9 -> x0, other arithmetic: 7.41 us -> none  [the longest x1 4.58 us: block_grads(): (prob_tile.astype(jnp.float32) * (dp_tile - row_delta) * softmax_scale).a...]
  transfers between devices with their start and end apart: 23 -> 0, of which waited for: 19 -> 0; matrix products, arithmetic and copies ran while one was open for 17% -> 0% of each run, Pallas kernels for 0% -> 0%
where the time goes in v1:
time: 112 us; the launch traced here: 110 us
  Pallas kernels  94.7 us (85%)
  local copies, waits for them, and re-layouts  14.5 us (13%)
    pallas_call x1, Pallas kernels, body(): pl.pallas_call(kernel, out_shape=(jax.ShapeDtypeStruct((128, 16, 128), BF...  94.7 us
    unnamed x10, local copies, waits for them, and re-layouts  14.5 us

profile of v1, /device:TPU:2, one launch (start us, length us, event | category | flops | bytes accessed | tf_op | source)
XLA Modules:
  0.0 109.8 jit_solution(1499712934742642603)
XLA Ops:
  0.6 1.7 %copy.10.lat_hbm = bf16[128,576]{1,0:T(8,128)(2,1)} copy(bf16[128,576]{0,1:T(8,128)(2,1)} %param.6) | data formatting | bytes 294912 | tf_op args[1]
  2.3 4.9 %copy.9.q_hbm = bf16[128,16,576]{2,1,0:T(8,128)(2,1)} copy(bf16[128,16,576]{0,2,1:T(8,128)(2,1)} %param.5) | data formatting | bytes 4718592 | tf_op args[0]
  7.3 94.7 %shard_map.84 = (bf16[128,16,128]{2,1,0:T(8,128)(2,1)}, bf16[128,16,576]{2,1,0:T(8,128)(2,1)}, bf16[128,576]{1,0:T(8,128)(2,1)}, f32[128,128]{1,0:T(8,128)}) custom-call(bf16[128,16,576]{2,1,0:T(8,128)(2,1)} %copy.9.q_hbm, bf16[128,576]{1,0:T(8,128)(2,1)} %copy.10.lat_hbm, s32[1,128]{1,0:T(1,128)} %bitcast.3, bf16[512,16,128]{2,1,0:T(8,128)(2,1)} %vup_hbm.1, ...), custom_call_target="tpu_custom_call" | custom-call | tf_op jit(solution)/shard_map/pallas_call | solution.py:605
  102.0 1.7 %copy.12 = bf16[128,576]{0,1:T(8,128)(2,1)} copy(bf16[128,576]{1,0:T(8,128)(2,1)} %get-tuple-element.14) | data formatting | bytes 294912
  103.7 0.0 copy-start
  103.7 0.0 copy-start.1
  103.7 4.7 %copy.11 = bf16[128,16,576]{0,2,1:T(8,128)(2,1)} copy(bf16[128,16,576]{2,1,0:T(8,128)(2,1)} %get-tuple-element.13) | data formatting | bytes 4718592
  108.4 0.0 copy-done
  108.4 0.8 copy.15
  109.2 0.0 copy-done.1
  109.2 0.6 copy.16
Async XLA Ops:
  103.7 4.7 %copy-start = (bf16[128,16,128]{2,1,0:T(8,128)(2,1)S(1)}, bf16[128,16,128]{2,1,0:T(8,128)(2,1)}, u32[]{:S(2)}) copy-start(bf16[128,16,128]{2,1,0:T(8,128)(2,1)} %get-tuple-element.20) | copy-start | bytes 1572868
  103.7 5.5 %copy-start.1 = (f32[128,128]{1,0:T(8,128)S(1)}, f32[128,128]{1,0:T(8,128)}, u32[]{:S(2)}) copy-start(f32[128,128]{1,0:T(8,128)} %get-tuple-element.11) | copy-start | bytes 196612

commit v2 on v1

--- a/solution.py
+++ b/solution.py
@@ -25,23 +25,14 @@
     return lax.dot_general(a, b, (((1,), (1,)), ((), ())), preferred_element_type=F32)
 
 
-def swap_halves(x):
-    lane = lax.broadcasted_iota(jnp.int32, x.shape, 1)
-    return jnp.where(lane < 32, pltpu.roll(x, 96, 1), pltpu.roll(x, 32, 1))
-
-
-def widened(x):
-    return jnp.concatenate([x, jnp.zeros_like(x)], axis=1)
-
-
 def kernel(
     q_hbm, lat_hbm, pos_ref, vup_hbm, cot_hbm,
     attn_hbm, gq_hbm, gl_hbm, gv_hbm,
-    q_raw, lat_raw, vup_raw, cot_raw, tab, sbuf, dpbuf, q_hm, q_t, do_hm, do_t, vup_h, cot_h,
-    p_buf, ds_buf, bias, ao, kw, k_t,
+    lat_raw, vup_raw, cot_raw, gq, tab, s_buf, dp_buf, q_t, do_t, vup_h, vup_t, cot_h,
+    p_buf, ds_buf, bias, peak, ao, kw, k_t,
     dup_s, rx, ry, xs, rxy, ys, ryx, zs, rz, gv,
-    dks, drow, zsend, zrecv, glt, gl,
-    in_sem, out_sem, kz_s, kz_r, kr_s, kr_r,
+    dks, drow, zsend, zrecv, glt,
+    in_sem, q_sem, out_sem, gq_sem, kz_s, kz_r, kr_s, kr_r,
     rx_s, rx_r, ry_s, ry_r, rxy_s, rxy_r, ryx_s, ryx_r, rz_s, rz_r,
     dr_s, dr_r, dz_s, dz_r, gl_s, gl_r,
 ):
@@ -63,12 +54,17 @@
 
     in_copies = [
         pltpu.make_async_copy(src, dst, in_sem.at[i])
-        for i, (src, dst) in enumerate(
-            ((lat_hbm, lat_raw), (vup_hbm, vup_raw), (cot_hbm, cot_raw), (q_hbm, q_raw))
-        )
+        for i, (src, dst) in enumerate(((lat_hbm, lat_raw), (vup_hbm, vup_raw), (cot_hbm, cot_raw)))
     ]
     for c in in_copies:
         c.start()
+
+    def q_copy(h):
+        cols = pl.ds(pl.multiple_of(h * 128, 128), 128)
+        return pltpu.make_async_copy(q_hbm.at[h], q_t.at[:, cols], q_sem.at[h])
+
+    for h in range(16):
+        q_copy(h).start()
 
     partners = []
     for t in range(1, 8):
@@ -87,22 +83,21 @@
         pl.semaphore_signal(barrier, inc=1, device_id=(c, h), device_id_type=MESH)
 
     lane = lax.broadcasted_iota(jnp.int32, (128, 128), 1)
-    freq_row = jnp.zeros((8, 128), F32)
-    lane8 = lax.broadcasted_iota(jnp.int32, (8, 128), 1) % 32
+    sub = lax.broadcasted_iota(jnp.int32, (128, 128), 0)
+    frequency = jnp.zeros((32, 128), F32)
     for i in range(32):
-        freq_row = jnp.where(lane8 == i, FREQUENCY[i], freq_row)
-    pos_col = jnp.broadcast_to(pos_ref[...].astype(F32), (128, 128)).T
-    angle = pos_col * freq_row[:1]
-    sine = jnp.where(lane < 32, -jnp.sin(angle), jnp.sin(angle))
-    tab[0] = jnp.where(lane < 64, jnp.cos(angle), 0.0)
-    tab[1] = jnp.where(lane < 64, sine, 0.0)
+        frequency = jnp.where(sub[:32] == i, FREQUENCY[i], frequency)
+    angle = pos_ref[...].astype(F32) * frequency
+    tab[0] = jnp.cos(angle)
+    tab[1] = jnp.sin(angle)
 
     in_copies[0].wait()
     own = 7 * 128
-    kw[own:own + 128, :512] = lat_raw[:, :512]
-    k_rope = widened(lat_raw[:, 512:].astype(F32))
-    k_rope = k_rope * tab[0] + swap_halves(k_rope) * tab[1]
-    kw[own:own + 128, 512:] = k_rope[:, :64].astype(BF16)
+    k_t[:512, own:own + 128] = lat_raw[:512, :]
+    lower, upper = lat_raw[512:544, :].astype(F32), lat_raw[544:576, :].astype(F32)
+    k_t[512:544, own:own + 128] = (lower * tab[0] - upper * tab[1]).astype(BF16)
+    k_t[544:576, own:own + 128] = (upper * tab[0] + lower * tab[1]).astype(BF16)
+    kw[own:own + 128, :] = k_t[:, own:own + 128].T
 
     pl.semaphore_wait(barrier, len(partners))
 
@@ -157,41 +152,31 @@
 
     def vup_in(i, c):
         v = vup_raw[pl.ds(i * 8, 8)].astype(F32).reshape(128, 128)
-        sbuf[i // 16, pl.ds((i % 16) * 128, 128), :] = v
+        s_buf[i // 8, pl.ds((i % 8) * 128, 128), :] = v
         return c
 
     def cot_in(i, c):
-        sbuf[4, pl.ds(i * 128, 128), :] = cot_raw[pl.ds(i * 8, 8)].astype(F32).reshape(128, 128)
-        return c
-
-    def q_in(i, c):
-        for j in range(5):
-            w = 128 if j < 4 else 64
-            x = q_raw[pl.ds(i * 8, 8), :, j * 128:j * 128 + w].astype(F32).reshape(128, w)
-            dpbuf[j, pl.ds(i * 128, 128), :] = x if w == 128 else widened(x)
+        s_buf[8 + i // 8, pl.ds((i % 8) * 128, 128), :] = cot_raw[pl.ds(i * 8, 8)].astype(F32).reshape(128, 128)
         return c
 
     def head_up(h, c):
-        rows = pl.ds(h * 128, 128)
-        for cc in range(4):
-            vup_h[h, cc * 128:(cc + 1) * 128, :] = sbuf[cc, pl.ds(h, 128, stride=16), :].astype(BF16)
-        cot = sbuf[4, pl.ds(h, 128, stride=16), :].astype(BF16)
+        for cc in range(8):
+            vup_h[h, cc * 64:(cc + 1) * 64, :] = s_buf[cc, pl.ds(h, 64, stride=16), :].astype(BF16)
+        cot = jnp.concatenate(
+            [s_buf[8, pl.ds(h, 64, stride=16), :], s_buf[9, pl.ds(h, 64, stride=16), :]], axis=0
+        ).astype(BF16)
         cot_h[h] = cot
         v = vup_h[h]
-        do_hm[rows, :] = dot_nt(cot, v).astype(BF16)
-        do_t[:, rows] = dot_nt(v, cot).astype(BF16)
+        vup_t[h] = v.T
+        do_t[:, pl.ds(pl.multiple_of(h * 128, 128), 128)] = dot(v, cot.T).astype(BF16)
         return c
 
     def head_q(h, c):
-        rows = pl.ds(h * 128, 128)
-        for j in range(4):
-            x = dpbuf[j, pl.ds(h, 128, stride=16), :].astype(BF16)
-            q_hm[rows, j * 128:(j + 1) * 128] = x
-            q_t[j * 128:(j + 1) * 128, rows] = x.T
-        x = dpbuf[4, pl.ds(h, 128, stride=16), :]
-        x = (x * tab[0] + swap_halves(x) * tab[1]).astype(BF16)
-        q_hm[rows, 512:576] = x[:, :64]
-        q_t[512:576, rows] = x.T[:64]
+        q_copy(h).wait()
+        cols = pl.ds(pl.multiple_of(h * 128, 128), 128)
+        lower, upper = q_t[512:544, cols].astype(F32), q_t[544:576, cols].astype(F32)
+        q_t[512:544, cols] = (lower * tab[0] - upper * tab[1]).astype(BF16)
+        q_t[544:576, cols] = (upper * tab[0] + lower * tab[1]).astype(BF16)
         return c
 
     in_copies[1].wait()
@@ -199,10 +184,9 @@
     in_copies[2].wait()
     lax.fori_loop(0, 16, cot_in, 0)
     forward(1)
-    lax.fori_loop(0, 16, head_up, 0)
+    lax.fori_loop(0, 8, head_up, 0)
     forward(2)
-    in_copies[3].wait()
-    lax.fori_loop(0, 16, q_in, 0)
+    lax.fori_loop(8, 16, head_up, 0)
     forward(3)
     lax.fori_loop(0, 16, head_q, 0)
 
@@ -212,28 +196,30 @@
         for t in range(1, 4):
             klast(t).start()
 
-    q_idx = lax.broadcasted_iota(jnp.int32, (128, 128), 0)
-    pos_row = pos_col.astype(jnp.int32)
     for w in range(8):
-        back = 896 - w * 128 + q_idx - lane
-        bias[:, w * 128:(w + 1) * 128] = jnp.where((back >= 0) & (back <= pos_row), 0.0, -jnp.inf)
+        back = 896 - w * 128 + lane - sub
+        bias[w * 128:(w + 1) * 128, :] = jnp.where((back >= 0) & (back <= pos_ref[...]), 0.0, -jnp.inf)
 
     def score_group(g):
-        cols = slice(g * 256, g * 256 + 256)
+        rows = slice(g * 256, g * 256 + 256)
+
+        def qk(r, c):
+            cols = pl.ds(pl.multiple_of(r * 512, 512), 512)
+            s = dot(kw[rows, :], q_t[:, cols])
+            d = dot(kw[rows, :512], do_t[:, cols])
+            for j in range(4):
+                h = r * 4 + j
+                x = s[:, j * 128:(j + 1) * 128] * (SCALE * LOG2E) + bias[rows, :]
+                s_buf[h, rows, :] = x
+                dp_buf[h, rows, :] = d[:, j * 128:(j + 1) * 128] * SCALE
+                top = jnp.max(x.reshape(32, 8, 128), axis=0)
+                peak[h] = top if g == 3 else jnp.maximum(peak[h], top)
+            return c
+
+        lax.fori_loop(0, 4, qk, 0)
         for w in (2 * g, 2 * g + 1):
-            k_t[:, w * 128:(w + 1) * 128] = kw[w * 128:(w + 1) * 128, :].T
-
-        def qk(r, c):
-            rows = pl.ds(r * 512, 512)
-            s = dot(q_hm[rows, :], k_t[:, cols])
-            sbuf[2 * g, rows, :] = s[:, :128]
-            sbuf[2 * g + 1, rows, :] = s[:, 128:]
-            s = dot(do_hm[rows, :], k_t[:512, cols])
-            dpbuf[2 * g, rows, :] = s[:, :128]
-            dpbuf[2 * g + 1, rows, :] = s[:, 128:]
-            return c
-
-        lax.fori_loop(0, 4, qk, 0)
+            if w < 7:
+                k_t[:, w * 128:(w + 1) * 128] = kw[w * 128:(w + 1) * 128, :].T
 
     def arrived(d):
         for t in range(1, 8):
@@ -331,39 +317,48 @@
         for j in range(4):
             gv[pl.ds(4 * hg + j, 8, stride=16), :] = total[8 * j:8 * j + 8]
 
+    def softmax(h, c):
+        cols = pl.ds(pl.multiple_of(h * 128, 128), 128)
+        top = jnp.max(peak[h], axis=0, keepdims=True)
+
+        def folded(x):
+            return jnp.sum(x.reshape(16, 8, 128), axis=0)
+
+        def block(i):
+            return pl.ds(pl.multiple_of(i * 128, 128), 128)
+
+        def exps(i, mass):
+            e = jnp.exp2(s_buf[h, block(i), :] - top)
+            s_buf[h, block(i), :] = e
+            return mass + folded(e)
+
+        mass = lax.fori_loop(0, 8, exps, jnp.zeros((8, 128), F32), unroll=2)
+        inverse = 1.0 / jnp.sum(mass, axis=0, keepdims=True)
+
+        def probs(i, delta):
+            p = (s_buf[h, block(i), :] * inverse).astype(BF16)
+            p_buf[block(i), cols] = p
+            return delta + folded(p.astype(F32) * dp_buf[h, block(i), :])
+
+        delta = lax.fori_loop(0, 8, probs, jnp.zeros((8, 128), F32), unroll=2)
+        delta = jnp.sum(delta, axis=0, keepdims=True)
+
+        def score_grads(i, c2):
+            p = p_buf[block(i), cols].astype(F32)
+            ds_buf[block(i), cols] = (p * (dp_buf[h, block(i), :] - delta)).astype(BF16)
+            return c2
+
+        lax.fori_loop(0, 8, score_grads, 0, unroll=2)
+        return c
+
     def group(hg, c):
-        def soft(r, c2):
-            q0 = pl.multiple_of((r % 4) * 32, 32)
-            rows = pl.ds(pl.multiple_of(hg * 512 + r * 32, 32), 32)
-            s = [sbuf[w, rows, :] + bias[pl.ds(q0, 32), w * 128:(w + 1) * 128] for w in range(8)]
-            m = s[0]
-            for w in range(1, 8):
-                m = jnp.maximum(m, s[w])
-            m = jnp.max(m, axis=1, keepdims=True)
-            e = [jnp.exp2((x - m) * (SCALE * LOG2E)) for x in s]
-            mass = e[0]
-            for w in range(1, 8):
-                mass = mass + e[w]
-            inverse = 1.0 / jnp.sum(mass, axis=1, keepdims=True)
-            p = [(x * inverse).astype(BF16) for x in e]
-            delta = jnp.zeros((32, 128), F32)
-            for w in range(8):
-                p_buf[rows, w * 128:(w + 1) * 128] = p[w]
-                delta = delta + p[w].astype(F32) * dpbuf[w, rows, :]
-            delta = jnp.sum(delta, axis=1, keepdims=True)
-            for w in range(8):
-                ds = p[w].astype(F32) * (dpbuf[w, rows, :] - delta) * SCALE
-                ds_buf[rows, w * 128:(w + 1) * 128] = ds.astype(BF16)
-            return c2
-
-        lax.fori_loop(0, 16, soft, 0)
-        rows = pl.ds(pl.multiple_of(hg * 512, 512), 512)
-        o = dot(p_buf[rows, :], kw[:, :512]).astype(BF16)
+        lax.fori_loop(4 * hg, 4 * hg + 4, softmax, 0)
+        o = dot(k_t[:512, :], p_buf[:, pl.ds(pl.multiple_of(hg * 512, 512), 512)]).astype(BF16)
         for j in range(4):
             h = hg * 4 + j
-            oh = o[j * 128:(j + 1) * 128]
-            ao[pl.ds(h, 128, stride=16), :] = dot(oh, vup_h[h])
-            up = dot(oh.T, cot_h[h]).reshape(32, 2, 8, 128)
+            oh = o[:, j * 128:(j + 1) * 128]
+            ao[pl.ds(h, 128, stride=16), :] = dot(vup_t[h], oh).T
+            up = dot(oh, cot_h[h]).reshape(32, 2, 8, 128)
             for half in range(2):
                 dup_s[h, half] = up[:, half].reshape(256, 128).astype(BF16)
         x_copy(hg).start()
@@ -413,9 +408,9 @@
         return a2 >= a
 
     def key_grads(g):
-        cols = slice(g * 256, g * 256 + 256)
-        x = dot(q_t[...], ds_buf[:, cols])
-        v = dot(do_t[...], p_buf[:, cols])
+        rows = slice(g * 256, g * 256 + 256)
+        x = dot_nt(q_t[...], ds_buf[rows, :])
+        v = dot_nt(do_t[...], p_buf[rows, :])
         for i in range(2):
             part = slice(128 * i, 128 * i + 128)
             dks[2 * g + i, :512, :] = (x[:512, part] + v[:, part]).astype(BF16)
@@ -427,7 +422,7 @@
         total = quarter(7 - 2 * d, head)[...].astype(F32)
         for t in range(1, 8):
             total = total + drow[d, (me + t) % 8].astype(F32)
-        zsend[d] = total.astype(BF16)
+        zsend[d] = total
         dz_copy(d).start()
 
     @pl.when(a == 1)
@@ -436,7 +431,7 @@
 
     @pl.when(a == 0)
     def _():
-        zrecv[4] = jnp.zeros((144, 128), BF16)
+        zrecv[4] = jnp.zeros((144, 128), F32)
 
     key_grads(0)
 
@@ -463,7 +458,7 @@
         total = drow[4, 0].astype(F32)
         for h2 in range(1, 4):
             total = total + drow[4, h2].astype(F32)
-        zsend[4] = total.astype(BF16)
+        zsend[4] = total
         dz_copy(4).start()
 
     key_grads(3)
@@ -475,17 +470,28 @@
             dr_copy(0, t).start()
     row_sum(2)
 
+    def gq_copy(h):
+        return pltpu.make_async_copy(gq.at[h], gq_hbm.at[h], gq_sem.at[h])
+
     def dq(r, c):
-        x = dot(ds_buf[pl.ds(pl.multiple_of(r * 512, 512), 512), :], kw[...])
+        x = dot(k_t[...], ds_buf[:, pl.ds(pl.multiple_of(r * 512, 512), 512)])
         for j in range(4):
             h = r * 4 + j
-            part = x[j * 128:(j + 1) * 128]
-            for t in range(4):
-                dpbuf[t, pl.ds(h, 128, stride=16), :] = part[:, t * 128:(t + 1) * 128]
-            rope = widened(part[:, 512:])
-            dpbuf[4, pl.ds(h, 128, stride=16), :] = rope * tab[0] - swap_halves(rope) * tab[1]
-        return c
-
+            part = x[:, j * 128:(j + 1) * 128]
+            lower, upper = part[512:544], part[544:576]
+            gq[h, :512, :] = part[:512].astype(BF16)
+            gq[h, 512:544, :] = (lower * tab[0] + upper * tab[1]).astype(BF16)
+            gq[h, 544:576, :] = (upper * tab[0] - lower * tab[1]).astype(BF16)
+            gq_copy(h).start()
+        return c
+
+    def attn16(i, c):
+        cot_raw[pl.ds(i * 8, 8)] = ao[pl.ds(i * 128, 128), :].reshape(8, 16, 128).astype(BF16)
+        return c
+
+    lax.fori_loop(0, 16, attn16, 0)
+    outs = [pltpu.make_async_copy(cot_raw, attn_hbm, out_sem.at[0])]
+    outs[0].start()
     lax.fori_loop(0, 2, dq, 0)
     row_sum(1)
 
@@ -494,6 +500,8 @@
         return c
 
     lax.fori_loop(0, 4, last, 0)
+    outs.append(pltpu.make_async_copy(gv, gv_hbm, out_sem.at[1]))
+    outs[-1].start()
     lax.fori_loop(2, 4, dq, 0)
 
     for t in range(1, 8):
@@ -511,10 +519,10 @@
         dz_copy(4).wait_recv()
 
     for d in (1, 2, 3, 4):
-        total = total + zrecv[d].astype(F32)
+        total = total + zrecv[d]
     roped = head == 3
-    cosine = jnp.where(roped, tab[0].T[:32], 1.0)
-    sine = jnp.where(roped, tab[1].T[32:64], 0.0)
+    cosine = jnp.where(roped, tab[0], 1.0)
+    sine = jnp.where(roped, tab[1], 0.0)
     lower, upper = total[80:112], total[112:144]
     own_quarter = glt.at[pl.ds(pl.multiple_of(144 * head, 16), 144)]
     own_quarter[...] = jnp.concatenate(
@@ -532,28 +540,9 @@
     for t in range(1, 4):
         gl_copy(t).start()
 
-    def out16(i, c):
-        toks = pl.ds(i * 8, 8)
-        cot_raw[toks] = ao[pl.ds(i * 128, 128), :].reshape(8, 16, 128).astype(BF16)
-        for j in range(5):
-            w = 128 if j < 4 else 64
-            part = dpbuf[j, pl.ds(i * 128, 128), :]
-            q_raw[toks, :, j * 128:j * 128 + w] = part[:, :w].reshape(8, 16, w).astype(BF16)
-        return c
-
-    outs = [pltpu.make_async_copy(gv, gv_hbm, out_sem.at[0])]
-    outs[0].start()
-    for i in range(4):
-        lax.fori_loop(4 * i, 4 * i + 4, out16, 0)
-        toks = pl.ds(32 * i, 32)
-        outs.append(pltpu.make_async_copy(q_raw.at[toks], gq_hbm.at[toks], out_sem.at[1 + i]))
-        outs[-1].start()
-    outs.append(pltpu.make_async_copy(cot_raw, attn_hbm, out_sem.at[5]))
-    outs[-1].start()
     for t in range(1, 4):
         gl_got(t).wait_recv()
-    gl[...] = glt[...].T
-    outs.append(pltpu.make_async_copy(gl, gl_hbm, out_sem.at[6]))
+    outs.append(pltpu.make_async_copy(glt, gl_hbm, out_sem.at[2]))
     outs[-1].start()
 
     for d in (1, 2, 3):
@@ -597,6 +586,8 @@
     lax.fori_loop(0, 4, drained, 0)
     for c in outs:
         c.wait()
+    for h in range(16):
+        gq_copy(h).wait()
 
 
 def body(queries, latent_kv, positions, value_up, cotangent):
@@ -606,26 +597,26 @@
         kernel,
         out_shape=(
             jax.ShapeDtypeStruct((128, 16, 128), BF16),
-            jax.ShapeDtypeStruct((128, 16, 576), BF16),
-            jax.ShapeDtypeStruct((128, 576), BF16),
+            jax.ShapeDtypeStruct((16, 576, 128), BF16),
+            jax.ShapeDtypeStruct((576, 128), BF16),
             jax.ShapeDtypeStruct((128, 128), F32),
         ),
         in_specs=[anywhere, anywhere, pl.BlockSpec(memory_space=pltpu.VMEM), anywhere, anywhere],
         out_specs=(anywhere,) * 4,
         scratch_shapes=[
-            vmem((128, 16, 576), BF16), vmem((128, 576), BF16), vmem((512, 16, 128), BF16),
-            vmem((128, 16, 128), BF16), vmem((2, 128, 128), F32),
-            vmem((8, 2048, 128), F32), vmem((8, 2048, 128), F32),
-            vmem((2048, 576), BF16), vmem((576, 2048), BF16), vmem((2048, 512), BF16), vmem((512, 2048), BF16),
-            vmem((16, 512, 128), BF16), vmem((16, 128, 128), BF16),
-            vmem((2048, 1024), BF16), vmem((2048, 1024), BF16), vmem((128, 1024), F32), vmem((2048, 128), F32),
-            vmem((1024, 576), BF16), vmem((576, 1024), BF16),
+            vmem((576, 128), BF16), vmem((512, 16, 128), BF16), vmem((128, 16, 128), BF16),
+            vmem((16, 576, 128), BF16), vmem((2, 32, 128), F32),
+            vmem((16, 1024, 128), F32), vmem((16, 1024, 128), F32),
+            vmem((576, 2048), BF16), vmem((512, 2048), BF16),
+            vmem((16, 512, 128), BF16), vmem((16, 128, 512), BF16), vmem((16, 128, 128), BF16),
+            vmem((1024, 2048), BF16), vmem((1024, 2048), BF16), vmem((1024, 128), F32), vmem((16, 8, 128), F32),
+            vmem((2048, 128), F32), vmem((1024, 576), BF16), vmem((576, 1024), BF16),
             vmem((16, 2, 256, 128), BF16), vmem((4, 2, 256, 128), BF16), vmem((4, 3, 2, 2, 64, 128), BF16),
             vmem((4, 2, 256, 128), F32), vmem((4, 3, 2, 64, 128), F32), vmem((4, 2, 2, 64, 128), F32),
             vmem((4, 2, 64, 128), F32), vmem((8, 128, 128), F32), vmem((7, 128, 128), F32), vmem((128, 128), F32),
-            vmem((8, 576, 128), BF16), vmem((5, 8, 144, 128), BF16), vmem((5, 144, 128), BF16),
-            vmem((5, 144, 128), BF16), vmem((576, 128), BF16), vmem((128, 576), BF16),
-            dma((4,)), dma((7,)), dma((5,)), dma((5,)), dma((5, 8)), dma((5, 8)),
+            vmem((8, 576, 128), BF16), vmem((5, 8, 144, 128), BF16), vmem((5, 144, 128), F32),
+            vmem((5, 144, 128), F32), vmem((576, 128), BF16),
+            dma((3,)), dma((16,)), dma((3,)), dma((16,)), dma((5,)), dma((5,)), dma((5, 8)), dma((5, 8)),
             dma((4,)), dma((4,)), dma((4, 3)), dma((4, 3)), dma((4, 3)), dma((4, 3)), dma((4,)), dma((4,)),
             dma((4, 7)), dma((4, 7)),
             dma((5, 8)), dma((5, 8)), dma((5,)), dma((5,)), dma((4,)), dma((4,)),
@@ -633,8 +624,10 @@
         compiler_params=pltpu.CompilerParams(
             collective_id=0, has_side_effects=True, vmem_limit_bytes=64 * 2**20 - 2**16
         ),
-    )(queries, latent_kv, positions.reshape(1, 128), value_up, cotangent)
-    return attn, gq, gl, gv.reshape(8, 16, 128)
+    )(
+        jnp.transpose(queries, (1, 2, 0)), latent_kv.T, positions.reshape(1, 128), value_up, cotangent
+    )
+    return attn, jnp.transpose(gq, (2, 0, 1)), gl.T, gv.reshape(8, 16, 128)
 
 
 def solution(mesh):

time: 112 us -> 96.2 us (0.86); the launches traced: 110 us -> 95.6 us
  local copies, waits for them, and re-layouts: 14.5 us -> 6.45 us
  Pallas kernels: 94.7 us -> 88.6 us
    unnamed x10 -> x8, local copies, waits for them, and re-layouts: 14.5 us -> 6.45 us
    pallas_call x1, Pallas kernels: 94.7 us -> 88.6 us  [body(): pl.pallas_call(kernel, out_shape=(jax.ShapeDtypeStruct((128, 16, 128), BF...]
where the time goes in v2:
time: 96.2 us; the launch traced here: 95.6 us
  Pallas kernels  88.6 us (92%)
  local copies, waits for them, and re-layouts  6.45 us (7%)
    pallas_call x1, Pallas kernels, body(): pl.pallas_call(kernel, out_shape=(jax.ShapeDtypeStruct((128, 16, 128), BF...  88.6 us
    unnamed x8, local copies, waits for them, and re-layouts  6.45 us

profile of v2, /device:TPU:2, one launch (start us, length us, event | category | flops | bytes accessed | tf_op | source)
XLA Modules:
  0.0 95.6 jit_solution(1075293440842010225)
XLA Ops:
  0.6 88.6 %shard_map.84 = (bf16[128,16,128]{2,1,0:T(8,128)(2,1)}, bf16[16,576,128]{2,1,0:T(8,128)(2,1)}, bf16[576,128]{1,0:T(8,128)(2,1)}, f32[128,128]{1,0:T(8,128)}) custom-call(bf16[16,576,128]{2,1,0:T(8,128)(2,1)} %bitcast.7, bf16[576,128]{1,0:T(8,128)(2,1)} %bitcast.9, s32[1,128]{1,0:T(1,128)} %bitcast.11, bf16[512,16,128]{2,1,0:T(8,128)(2,1)} %vup_hbm.1, ...), custom_call_target="tpu_custom_call" | custom-call | tf_op jit(solution)/shard_map/pallas_call | solution.py:596
  89.2 1.9 %copy.13 = bf16[128,16,128]{2,1,0:T(8,128)(2,1)} copy(bf16[128,16,128]{2,1,0:T(8,128)(2,1)} %get-tuple-element.16) | data formatting | bytes 1048576
  91.1 0.0 copy-start
  91.1 0.0 copy-start.1
  91.1 3.3 %copy.14 = bf16[128,16,576]{0,2,1:T(8,128)(2,1)} copy(bf16[128,16,576]{0,2,1:T(8,128)(2,1)} %bitcast.6) | data formatting | bytes 4718592
  94.3 0.0 copy-done
  94.3 0.7 copy.15
  95.0 0.0 copy-done.1
  95.0 0.6 copy.16
Async XLA Ops:
  91.1 3.3 %copy-start = (bf16[576,128]{1,0:T(8,128)(2,1)S(1)}, bf16[576,128]{1,0:T(8,128)(2,1)}, u32[]{:S(2)}) copy-start(bf16[576,128]{1,0:T(8,128)(2,1)} %get-tuple-element.10) | copy-start | bytes 442372
  91.1 3.9 %copy-start.1 = (f32[128,128]{1,0:T(8,128)S(1)}, f32[128,128]{1,0:T(8,128)}, u32[]{:S(2)}) copy-start(f32[128,128]{1,0:T(8,128)} %get-tuple-element.11) | copy-start | bytes 196612

commit v3 on v2

--- a/solution.py
+++ b/solution.py
@@ -30,10 +30,10 @@
     attn_hbm, gq_hbm, gl_hbm, gv_hbm,
     lat_raw, vup_raw, cot_raw, gq, tab, s_buf, dp_buf, q_t, do_t, vup_h, vup_t, cot_h,
     p_buf, ds_buf, bias, peak, ao, kw, k_t,
-    dup_s, rx, ry, xs, rxy, ys, ryx, zs, rz, gv,
+    o_buf, ox, oy, cotx, coty, dxf, xs, rxy, ysf, ysb, ryx, zs, rz, fxs, fxr, fys, fyr, gv,
     dks, drow, zsend, zrecv, glt,
     in_sem, q_sem, out_sem, gq_sem, kz_s, kz_r, kr_s, kr_r,
-    rx_s, rx_r, ry_s, ry_r, rxy_s, rxy_r, ryx_s, ryx_r, rz_s, rz_r,
+    cx_s, cx_r, cy_s, cy_r, ox_s, ox_r, oy_s, oy_r, xy_s, xy_r, yx_s, yx_r, rz_s, rz_r, fx_s, fx_r, fy_s, fy_r,
     dr_s, dr_r, dz_s, dz_r, gl_s, gl_r,
 ):
     ctx, head = lax.axis_index("ctx"), lax.axis_index("head")
@@ -188,6 +188,40 @@
     forward(2)
     lax.fori_loop(8, 16, head_up, 0)
     forward(3)
+
+    def cx_copy(hg):
+        return rcopy(
+            cot_h.at[4 * hg + 1 - a], cotx.at[hg, pl.ds(pl.multiple_of(128 * a, 128), 128)],
+            cx_s.at[hg], cx_r.at[hg], partner, head,
+        )
+
+    def cx_got(hg):
+        ref = cotx.at[hg, pl.ds(pl.multiple_of(128 - 128 * a, 128), 128)]
+        return rcopy(ref, ref, cx_s.at[hg], cx_r.at[hg], partner, head)
+
+    def y_head(r, y2):
+        return 4 * (2 * r + y2 // 2) + 2 + y2 % 2
+
+    def cy_copy(r, t):
+        y2 = (y + t) % 4
+        return rcopy(
+            cot_h.at[y_head(r, y2)], coty.at[r, pl.ds(pl.multiple_of(128 * y, 128), 128)],
+            cy_s.at[r, t], cy_r.at[r, y], y2 * 16 + ctx % 16, head,
+        )
+
+    def cy_got(r, t):
+        y2 = (y + t) % 4
+        ref = coty.at[r, pl.ds(pl.multiple_of(128 * y2, 128), 128)]
+        return rcopy(ref, ref, cy_s.at[r, t], cy_r.at[r, y2], y2 * 16 + ctx % 16, head)
+
+    for hg in range(4):
+        cx_copy(hg).start()
+        cotx[hg, pl.ds(pl.multiple_of(128 * a, 128), 128), :] = cot_h[4 * hg + a]
+    for r in range(2):
+        for t in range(1, 4):
+            cy_copy(r, t).start()
+        coty[r, pl.ds(pl.multiple_of(128 * y, 128), 128), :] = cot_h[y_head(r, y)]
+
     lax.fori_loop(0, 16, head_q, 0)
 
     @pl.when(a == 0)
@@ -204,14 +238,11 @@
         rows = slice(g * 256, g * 256 + 256)
 
         def qk(r, c):
-            cols = pl.ds(pl.multiple_of(r * 512, 512), 512)
-            s = dot(kw[rows, :], q_t[:, cols])
-            d = dot(kw[rows, :512], do_t[:, cols])
+            s = dot(kw[rows, :], q_t[:, pl.ds(pl.multiple_of(r * 512, 512), 512)])
             for j in range(4):
                 h = r * 4 + j
                 x = s[:, j * 128:(j + 1) * 128] * (SCALE * LOG2E) + bias[rows, :]
                 s_buf[h, rows, :] = x
-                dp_buf[h, rows, :] = d[:, j * 128:(j + 1) * 128] * SCALE
                 top = jnp.max(x.reshape(32, 8, 128), axis=0)
                 peak[h] = top if g == 3 else jnp.maximum(peak[h], top)
             return c
@@ -244,88 +275,125 @@
 
     score_group(0)
 
-    def x_copy(hg):
-        return rcopy(dup_s.at[pl.ds(4 * hg, 2), 1 - a], rx.at[hg], rx_s.at[hg], rx_r.at[hg], partner, head)
-
-    def y_to(t):
-        return ((y + t) % 4) * 16 + ctx % 16
-
-    def y_copy(hg, t):
+    def y_index(y2):
+        return y2 * 16 + ctx % 16
+
+    def ox_copy(hg):
+        cols = pl.ds(pl.multiple_of(128 * a, 128), 128)
+        return rcopy(o_buf.at[4 * hg + 1 - a], ox.at[hg, :, cols], ox_s.at[hg], ox_r.at[hg], partner, head)
+
+    def ox_got(hg):
+        ref = ox.at[hg, :, pl.ds(pl.multiple_of(128 - 128 * a, 128), 128)]
+        return rcopy(ref, ref, ox_s.at[hg], ox_r.at[hg], partner, head)
+
+    def oy_copy(hg, j):
+        y2 = 2 * (hg % 2) + j
+        cols = pl.ds(pl.multiple_of(128 * y, 128), 128)
+        return rcopy(
+            o_buf.at[4 * hg + 2 + j], oy.at[hg // 2, :, cols], oy_s.at[hg, j], oy_r.at[hg // 2, y],
+            y_index(y2), head,
+        )
+
+    def oy_got(r, t):
         y2 = (y + t) % 4
-        return rcopy(
-            dup_s.at[pl.ds(4 * hg + 2, 2), :, pl.ds(pl.multiple_of(64 * y2, 64), 64)], ry.at[hg, t - 1],
-            ry_s.at[hg, t - 1], ry_r.at[hg, t - 1], y_to(t), head,
-        )
+        ref = oy.at[r, :, pl.ds(pl.multiple_of(128 * y2, 128), 128)]
+        return rcopy(ref, ref, oy_s.at[2 * r, 0], oy_r.at[r, y2], y_index(y2), head)
 
     def xy_copy(hg, t):
         y2 = (y + t) % 4
+        rows = pl.ds(pl.multiple_of(128 * y2, 128), 128)
         return rcopy(
-            xs.at[hg, :, pl.ds(pl.multiple_of(64 * y2, 64), 64)], rxy.at[hg, t - 1],
-            rxy_s.at[hg, t - 1], rxy_r.at[hg, t - 1], y_to(t), head,
+            xs.at[hg, rows], rxy.at[hg, t - 1], xy_s.at[hg, t - 1], xy_r.at[hg, t - 1], y_index(y2), head
         )
 
-    def yx_copy(hg):
-        return rcopy(ys.at[hg, :, 1 - a], ryx.at[hg], ryx_s.at[hg], ryx_r.at[hg], partner, head)
-
-    def z_copy(hg, t):
+    def yx_copy(r):
+        return rcopy(ysb.at[r, 1 - a], ryx.at[r], yx_s.at[r], yx_r.at[r], partner, head)
+
+    def z_copy(r, t):
         z2 = (z + t) % 8
-        rows = pl.ds(pl.multiple_of(32 * hg, 32), 32)
         return rcopy(
-            zs.at[z2, rows], rz.at[t - 1, rows], rz_s.at[hg, t - 1], rz_r.at[hg, t - 1],
-            y * 16 + z2 * 2 + a, head,
+            zs.at[r, z2], rz.at[r, t - 1], rz_s.at[r, t - 1], rz_r.at[r, t - 1], y * 16 + z2 * 2 + a, head
         )
 
-    own_y = pl.ds(pl.multiple_of(64 * y, 64), 64)
-
-    def up_second(hg):
-        x_copy(hg).wait_recv()
+    def fx_copy(r):
+        return rcopy(fxs.at[r], fxr.at[r], fx_s.at[r], fx_r.at[r], partner, head)
+
+    def fy_copy(r, t):
+        y2 = (y + t) % 4
+        rows = pl.ds(pl.multiple_of(8 * y2, 8), 8)
+        return rcopy(fys.at[r, rows], fyr.at[r, t - 1], fy_s.at[r, t - 1], fy_r.at[r, t - 1], y_index(y2), head)
+
+    def x_second(hg):
+        ox_got(hg).wait_recv()
+        cx_got(hg).wait_recv()
+        total = dot(ox[hg], cotx[hg])
+        dxf[hg] = total
+        xs[hg] = total.astype(BF16)
+        for t in range(1, 4):
+            xy_copy(hg, t).start()
+
+    def y_second(r):
+        for t in range(1, 4):
+            oy_got(r, t).wait_recv()
+            cy_got(r, t).wait_recv()
+        total = dot(oy[r], coty[r]).reshape(32, 2, 8, 128)
+        for half in range(2):
+            part = total[:, half].reshape(256, 128)
+            ysf[r, half] = part
+            ysb[r, half] = part.astype(BF16)
+        yx_copy(r).start()
+
+    def third(r):
         for j in range(2):
-            xs[hg, j] = dup_s[4 * hg + j, a].astype(F32) + rx[hg, j].astype(F32)
-        for t in range(1, 4):
-            xy_copy(hg, t).start()
-        for t in range(1, 4):
-            y_copy(hg, t).wait_recv()
+            hg = 2 * r + j
+            for t in range(1, 4):
+                xy_copy(hg, t).wait_recv()
+            total = dxf[hg, pl.ds(pl.multiple_of(128 * y, 128), 128), :]
+            for t in range(3):
+                total = total + rxy[hg, t].astype(F32)
+            zs[r, :, 16 * j:16 * j + 16, :] = total.reshape(8, 16, 128)
+        yx_copy(r).wait_recv()
+        total = (ysf[r, a] + ryx[r].astype(F32)).reshape(4, 8, 8, 128)
+        for y2 in range(4):
+            zs[r, :, 32 + 8 * y2:40 + 8 * y2, :] = total[y2]
+        for t in range(1, 8):
+            z_copy(r, t).start()
+
+    def fourth(r):
+        for t in range(1, 8):
+            z_copy(r, t).wait_recv()
+        total = zs[r, z]
+        for t in range(7):
+            total = total + rz[r, t]
         for j in range(2):
-            for half in range(2):
-                total = dup_s[4 * hg + 2 + j, half, own_y, :].astype(F32)
-                for t in range(3):
-                    total = total + ry[hg, t, j, half].astype(F32)
-                ys[hg, j, half] = total
-        yx_copy(hg).start()
-
-    def up_third(hg):
-        for t in range(1, 4):
-            xy_copy(hg, t).wait_recv()
-        yx_copy(hg).wait_recv()
+            low, high = total[16 * j:16 * j + 8], total[16 * j + 8:16 * j + 16]
+            fxs[r, 8 * j:8 * j + 8, :] = jnp.where(a == 0, high, low)
+            gv[pl.ds(4 * (2 * r + j) + a, 8, stride=16), :] = jnp.where(a == 0, low, high)
+        fys[r] = total[32:]
+        fx_copy(r).start()
+        for t in range(1, 4):
+            fy_copy(r, t).start()
+
+    def fifth(r):
+        fx_copy(r).wait_recv()
         for j in range(2):
-            total = xs[hg, j, own_y, :]
-            for t in range(3):
-                total = total + rxy[hg, t, j]
-            zs[:, pl.ds(pl.multiple_of((4 * hg + j) * 8, 8), 8), :] = total.reshape(8, 8, 128)
-            total = ys[hg, j, a] + ryx[hg, j]
-            zs[:, pl.ds(pl.multiple_of((4 * hg + 2 + j) * 8, 8), 8), :] = total.reshape(8, 8, 128)
-        for t in range(1, 8):
-            z_copy(hg, t).start()
-
-    def up_last(hg):
-        for t in range(1, 8):
-            z_copy(hg, t).wait_recv()
-        rows = pl.ds(pl.multiple_of(32 * hg, 32), 32)
-        total = zs[z, rows, :]
-        for t in range(7):
-            total = total + rz[t, rows, :]
-        for j in range(4):
-            gv[pl.ds(4 * hg + j, 8, stride=16), :] = total[8 * j:8 * j + 8]
+            gv[pl.ds(4 * (2 * r + j) + 1 - a, 8, stride=16), :] = fxr[r, 8 * j:8 * j + 8, :]
+        for t in range(1, 4):
+            fy_copy(r, t).wait_recv()
+        for t in range(4):
+            y2 = (y + 4 - t) % 4
+            rows = fys[r, pl.ds(pl.multiple_of(8 * y, 8), 8), :] if t == 0 else fyr[r, t - 1]
+            gv[pl.ds(4 * (2 * r + y2 // 2) + 2 + y2 % 2, 8, stride=16), :] = rows
+
+    def folded(x):
+        return jnp.sum(x.reshape(16, 8, 128), axis=0)
+
+    def block(i):
+        return pl.ds(pl.multiple_of(i * 128, 128), 128)
 
     def softmax(h, c):
         cols = pl.ds(pl.multiple_of(h * 128, 128), 128)
         top = jnp.max(peak[h], axis=0, keepdims=True)
-
-        def folded(x):
-            return jnp.sum(x.reshape(16, 8, 128), axis=0)
-
-        def block(i):
-            return pl.ds(pl.multiple_of(i * 128, 128), 128)
 
         def exps(i, mass):
             e = jnp.exp2(s_buf[h, block(i), :] - top)
@@ -335,47 +403,77 @@
         mass = lax.fori_loop(0, 8, exps, jnp.zeros((8, 128), F32), unroll=2)
         inverse = 1.0 / jnp.sum(mass, axis=0, keepdims=True)
 
-        def probs(i, delta):
-            p = (s_buf[h, block(i), :] * inverse).astype(BF16)
-            p_buf[block(i), cols] = p
-            return delta + folded(p.astype(F32) * dp_buf[h, block(i), :])
-
-        delta = lax.fori_loop(0, 8, probs, jnp.zeros((8, 128), F32), unroll=2)
-        delta = jnp.sum(delta, axis=0, keepdims=True)
-
-        def score_grads(i, c2):
-            p = p_buf[block(i), cols].astype(F32)
-            ds_buf[block(i), cols] = (p * (dp_buf[h, block(i), :] - delta)).astype(BF16)
+        def probs(i, c2):
+            p_buf[block(i), cols] = (s_buf[h, block(i), :] * inverse).astype(BF16)
             return c2
 
-        lax.fori_loop(0, 8, score_grads, 0, unroll=2)
+        lax.fori_loop(0, 8, probs, 0, unroll=2)
         return c
 
-    def group(hg, c):
+    for hg in range(4):
         lax.fori_loop(4 * hg, 4 * hg + 4, softmax, 0)
-        o = dot(k_t[:512, :], p_buf[:, pl.ds(pl.multiple_of(hg * 512, 512), 512)]).astype(BF16)
+        o = dot(k_t[:512, :], p_buf[:, hg * 512:hg * 512 + 512]).astype(BF16)
+        for j in range(4):
+            o_buf[4 * hg + j] = o[:, j * 128:(j + 1) * 128]
+        ox_copy(hg).start()
+        ox[hg, :, pl.ds(pl.multiple_of(128 * a, 128), 128)] = o_buf[4 * hg + a]
+        for j in range(2):
+            @pl.when(y != 2 * (hg % 2) + j)
+            def _():
+                oy_copy(hg, j).start()
+
+            @pl.when(y == 2 * (hg % 2) + j)
+            def _():
+                oy[hg // 2, :, pl.ds(pl.multiple_of(128 * y, 128), 128)] = o_buf[4 * hg + 2 + j]
         for j in range(4):
             h = hg * 4 + j
-            oh = o[:, j * 128:(j + 1) * 128]
-            ao[pl.ds(h, 128, stride=16), :] = dot(vup_t[h], oh).T
-            up = dot(oh, cot_h[h]).reshape(32, 2, 8, 128)
-            for half in range(2):
-                dup_s[h, half] = up[:, half].reshape(256, 128).astype(BF16)
-        x_copy(hg).start()
-        for t in range(1, 4):
-            y_copy(hg, t).start()
-
-        @pl.when(hg >= 1)
-        def _():
-            up_second(hg - 1)
-
-        @pl.when(hg >= 2)
-        def _():
-            up_third(hg - 2)
-
+            ao[pl.ds(h, 128, stride=16), :] = dot(vup_t[h], o[:, j * 128:(j + 1) * 128]).T
+        if hg >= 1:
+            x_second(hg - 1)
+        if hg == 2:
+            y_second(0)
+
+    def attn16(i, c):
+        cot_raw[pl.ds(i * 8, 8)] = ao[pl.ds(i * 128, 128), :].reshape(8, 16, 128).astype(BF16)
         return c
 
-    lax.fori_loop(0, 4, group, 0)
+    lax.fori_loop(0, 16, attn16, 0)
+    outs = [pltpu.make_async_copy(cot_raw, attn_hbm, out_sem.at[0])]
+    outs[0].start()
+
+    def score_grads(hg):
+        dp_buf[...] = dot(kw[:, :512], do_t[:, hg * 512:hg * 512 + 512]) * SCALE
+
+        def one_head(j, c):
+            h = hg * 4 + j
+            cols = pl.ds(pl.multiple_of(h * 128, 128), 128)
+            dp_cols = pl.ds(pl.multiple_of(j * 128, 128), 128)
+
+            def deltas(i, delta):
+                return delta + folded(p_buf[block(i), cols].astype(F32) * dp_buf[block(i), dp_cols])
+
+            delta = lax.fori_loop(0, 8, deltas, jnp.zeros((8, 128), F32), unroll=2)
+            delta = jnp.sum(delta, axis=0, keepdims=True)
+
+            def grads(i, c2):
+                p = p_buf[block(i), cols].astype(F32)
+                ds_buf[block(i), cols] = (p * (dp_buf[block(i), dp_cols] - delta)).astype(BF16)
+                return c2
+
+            lax.fori_loop(0, 8, grads, 0, unroll=2)
+            return c
+
+        lax.fori_loop(0, 4, one_head, 0)
+
+    score_grads(0)
+    x_second(3)
+    y_second(1)
+    third(0)
+    score_grads(1)
+    score_grads(2)
+    third(1)
+    score_grads(3)
+    fourth(0)
 
     def quarter(slot, j):
         return dks.at[slot, pl.ds(pl.multiple_of(144 * j, 16), 144)]
@@ -440,12 +538,9 @@
         for h2 in range(4):
             dr_last(h2).start()
 
-    up_second(3)
-    up_third(2)
     key_grads(1)
     for t in range(1, 8):
         dr_copy(3, t).start()
-    up_third(3)
     key_grads(2)
     for t in range(1, 8):
         dr_copy(2, t).start()
@@ -485,23 +580,11 @@
             gq_copy(h).start()
         return c
 
-    def attn16(i, c):
-        cot_raw[pl.ds(i * 8, 8)] = ao[pl.ds(i * 128, 128), :].reshape(8, 16, 128).astype(BF16)
-        return c
-
-    lax.fori_loop(0, 16, attn16, 0)
-    outs = [pltpu.make_async_copy(cot_raw, attn_hbm, out_sem.at[0])]
-    outs[0].start()
     lax.fori_loop(0, 2, dq, 0)
     row_sum(1)
 
-    def last(hg, c):
-        up_last(hg)
-        return c
-
-    lax.fori_loop(0, 4, last, 0)
-    outs.append(pltpu.make_async_copy(gv, gv_hbm, out_sem.at[1]))
-    outs[-1].start()
+    fourth(1)
+    fifth(0)
     lax.fori_loop(2, 4, dq, 0)
 
     for t in range(1, 8):
@@ -539,6 +622,9 @@
 
     for t in range(1, 4):
         gl_copy(t).start()
+    fifth(1)
+    outs.append(pltpu.make_async_copy(gv, gv_hbm, out_sem.at[1]))
+    outs[-1].start()
 
     for t in range(1, 4):
         gl_got(t).wait_recv()
@@ -573,17 +659,23 @@
     for t in range(1, 4):
         gl_copy(t).wait_send()
 
-    def drained(hg, c):
-        x_copy(hg).wait_send()
-        yx_copy(hg).wait_send()
-        for t in range(1, 4):
-            y_copy(hg, t).wait_send()
+    for hg in range(4):
+        cx_copy(hg).wait_send()
+        ox_copy(hg).wait_send()
+        for t in range(1, 4):
             xy_copy(hg, t).wait_send()
+        for j in range(2):
+            @pl.when(y != 2 * (hg % 2) + j)
+            def _():
+                oy_copy(hg, j).wait_send()
+    for r in range(2):
+        yx_copy(r).wait_send()
+        fx_copy(r).wait_send()
+        for t in range(1, 4):
+            cy_copy(r, t).wait_send()
+            fy_copy(r, t).wait_send()
         for t in range(1, 8):
-            z_copy(hg, t).wait_send()
-        return c
-
-    lax.fori_loop(0, 4, drained, 0)
+            z_copy(r, t).wait_send()
     for c in outs:
         c.wait()
     for h in range(16):
@@ -606,19 +698,23 @@
         scratch_shapes=[
             vmem((576, 128), BF16), vmem((512, 16, 128), BF16), vmem((128, 16, 128), BF16),
             vmem((16, 576, 128), BF16), vmem((2, 32, 128), F32),
-            vmem((16, 1024, 128), F32), vmem((16, 1024, 128), F32),
+            vmem((16, 1024, 128), F32), vmem((1024, 512), F32),
             vmem((576, 2048), BF16), vmem((512, 2048), BF16),
             vmem((16, 512, 128), BF16), vmem((16, 128, 512), BF16), vmem((16, 128, 128), BF16),
             vmem((1024, 2048), BF16), vmem((1024, 2048), BF16), vmem((1024, 128), F32), vmem((16, 8, 128), F32),
             vmem((2048, 128), F32), vmem((1024, 576), BF16), vmem((576, 1024), BF16),
-            vmem((16, 2, 256, 128), BF16), vmem((4, 2, 256, 128), BF16), vmem((4, 3, 2, 2, 64, 128), BF16),
-            vmem((4, 2, 256, 128), F32), vmem((4, 3, 2, 64, 128), F32), vmem((4, 2, 2, 64, 128), F32),
-            vmem((4, 2, 64, 128), F32), vmem((8, 128, 128), F32), vmem((7, 128, 128), F32), vmem((128, 128), F32),
+            vmem((16, 512, 128), BF16), vmem((4, 512, 256), BF16), vmem((2, 512, 512), BF16),
+            vmem((4, 256, 128), BF16), vmem((2, 512, 128), BF16), vmem((4, 512, 128), F32), vmem((4, 512, 128), BF16),
+            vmem((4, 3, 128, 128), BF16), vmem((2, 2, 256, 128), F32), vmem((2, 2, 256, 128), BF16),
+            vmem((2, 256, 128), BF16), vmem((2, 8, 64, 128), F32), vmem((2, 7, 64, 128), F32),
+            vmem((2, 16, 128), F32), vmem((2, 16, 128), F32), vmem((2, 32, 128), F32), vmem((2, 3, 8, 128), F32),
+            vmem((128, 128), F32),
             vmem((8, 576, 128), BF16), vmem((5, 8, 144, 128), BF16), vmem((5, 144, 128), F32),
             vmem((5, 144, 128), F32), vmem((576, 128), BF16),
             dma((3,)), dma((16,)), dma((3,)), dma((16,)), dma((5,)), dma((5,)), dma((5, 8)), dma((5, 8)),
-            dma((4,)), dma((4,)), dma((4, 3)), dma((4, 3)), dma((4, 3)), dma((4, 3)), dma((4,)), dma((4,)),
-            dma((4, 7)), dma((4, 7)),
+            dma((4,)), dma((4,)), dma((2, 4)), dma((2, 4)), dma((4,)), dma((4,)), dma((4, 2)), dma((2, 4)),
+            dma((4, 3)), dma((4, 3)), dma((2,)), dma((2,)), dma((2, 7)), dma((2, 7)), dma((2,)), dma((2,)),
+            dma((2, 3)), dma((2, 3)),
             dma((5, 8)), dma((5, 8)), dma((5,)), dma((5,)), dma((4,)), dma((4,)),
         ],
         compiler_params=pltpu.CompilerParams(

time: 96.2 us -> 103 us (1.071)
  the two profiles are of different devices: /device:TPU:2 before, /device:TPU:27 now
where the time goes in v3:
time: 103 us
  Pallas kernels  96 us (93%)
  local copies, waits for them, and re-layouts  6.45 us (6%)
    pallas_call x1, Pallas kernels, body(): pl.pallas_call(kernel, out_shape=(jax.ShapeDtypeStruct((128, 16, 128), BF...  96 us
    unnamed x8, local copies, waits for them, and re-layouts  6.45 us

profile of v3, /device:TPU:27, one launch (start us, length us, event | category | flops | bytes accessed | tf_op | source)
XLA Modules:
  0.0 103.1 jit_solution(14060360972216117242)
XLA Ops:
  0.6 96.0 %shard_map.84 = (bf16[128,16,128]{2,1,0:T(8,128)(2,1)}, bf16[16,576,128]{2,1,0:T(8,128)(2,1)}, bf16[576,128]{1,0:T(8,128)(2,1)}, f32[128,128]{1,0:T(8,128)}) custom-call(bf16[16,576,128]{2,1,0:T(8,128)(2,1)} %bitcast.7, bf16[576,128]{1,0:T(8,128)(2,1)} %bitcast.9, s32[1,128]{1,0:T(1,128)} %bitcast.11, bf16[512,16,128]{2,1,0:T(8,128)(2,1)} %vup_hbm.1, ...), custom_call_target="tpu_custom_call" | custom-call | tf_op jit(solution)/shard_map/pallas_call | solution.py:688
  96.6 1.9 %copy.13 = bf16[128,16,128]{2,1,0:T(8,128)(2,1)} copy(bf16[128,16,128]{2,1,0:T(8,128)(2,1)} %get-tuple-element.16) | data formatting | bytes 1048576
  98.5 0.0 copy-start
  98.5 0.0 copy-start.1
  98.5 3.3 %copy.14 = bf16[128,16,576]{0,2,1:T(8,128)(2,1)} copy(bf16[128,16,576]{0,2,1:T(8,128)(2,1)} %bitcast.6) | data formatting | bytes 4718592
  101.8 0.0 copy-done
  101.8 0.7 copy.15
  102.4 0.0 copy-done.1
  102.4 0.6 copy.16
Async XLA Ops:
  98.5 3.3 %copy-start = (bf16[576,128]{1,0:T(8,128)(2,1)S(1)}, bf16[576,128]{1,0:T(8,128)(2,1)}, u32[]{:S(2)}) copy-start(bf16[576,128]{1,0:T(8,128)(2,1)} %get-tuple-element.10) | copy-start | bytes 442372
  98.5 3.9 %copy-start.1 = (f32[128,128]{1,0:T(8,128)S(1)}, f32[128,128]{1,0:T(8,128)}, u32[]{:S(2)}) copy-start(f32[128,128]{1,0:T(8,128)} %get-tuple-element.11) | copy-start | bytes 196612

commit v4 on v3

--- a/solution.py
+++ b/solution.py
@@ -29,22 +29,17 @@
     q_hbm, lat_hbm, pos_ref, vup_hbm, cot_hbm,
     attn_hbm, gq_hbm, gl_hbm, gv_hbm,
     lat_raw, vup_raw, cot_raw, gq, tab, s_buf, dp_buf, q_t, do_t, vup_h, vup_t, cot_h,
-    p_buf, ds_buf, bias, peak, ao, kw, k_t,
+    p_buf, ds_buf, bias, peak, ao, kw, k_t, k4,
     o_buf, ox, oy, cotx, coty, dxf, xs, rxy, ysf, ysb, ryx, zs, rz, fxs, fxr, fys, fyr, gv,
-    dks, drow, zsend, zrecv, glt,
-    in_sem, q_sem, out_sem, gq_sem, kz_s, kz_r, kr_s, kr_r,
+    dks, dcore, csf, csb, drow, zsend, zrecv, glt,
+    in_sem, q_sem, out_sem, gq_sem, ring_sem, kz_s, kz_r, kx_s, kx_r, kc_s, kc_r,
     cx_s, cx_r, cy_s, cy_r, ox_s, ox_r, oy_s, oy_r, xy_s, xy_r, yx_s, yx_r, rz_s, rz_r, fx_s, fx_r, fy_s, fy_r,
-    dr_s, dr_r, dz_s, dz_r, gl_s, gl_r,
+    dc_s, dc_r, dx_s, dx_r, dz_s, dz_r, gl_s, gl_r,
 ):
     ctx, head = lax.axis_index("ctx"), lax.axis_index("head")
     a, row = ctx % 2, ctx // 2
     y, z = ctx // 16, (ctx // 2) % 8
-    me = a * 4 + head
     partner = ctx + 1 - 2 * a
-
-    def mate(t):
-        m = (me + t) % 8
-        return m, m // 4, m % 4
 
     def rcopy(src, dst, ss, rs, to_ctx, to_head):
         return pltpu.make_async_remote_copy(
@@ -66,18 +61,26 @@
     for h in range(16):
         q_copy(h).start()
 
-    partners = []
-    for t in range(1, 8):
-        m, a2, h2 = mate(t)
-        partners.append((row * 2 + a2, h2))
-    for d in (1, 2, 3, 4):
-        partners.append(((ctx + 2 * d) % 64, head))
-        partners.append(((ctx + 64 - 2 * d) % 64, head))
-    partners.append(((ctx + 64 - 7 + 14 * a) % 64, head))
-    for t in range(1, 4):
-        partners.append((((y + t) % 4) * 16 + ctx % 16, head))
-    for t in range(1, 8):
-        partners.append((y * 16 + ((z + t) % 8) * 2 + a, head))
+    core, chip = head % 2, (head // 2) * 2 + a
+
+    def chip_at(t):
+        x2 = (chip + t) % 4
+        return x2, x2 % 2, x2 // 2
+
+    def on_chip(t):
+        x2, a2, hi2 = chip_at(t)
+        return row * 2 + a2, hi2 * 2 + core
+
+    def y_index(y2):
+        return (y2 % 4) * 16 + ctx % 16
+
+    def z_index(z2):
+        return y * 16 + (z2 % 8) * 2 + a
+
+    sibling = head + 1 - 2 * core
+    up_row, down_row = (ctx + 2) % 64, (ctx + 62) % 64
+    rings = [(y_index(y + 1), head), (y_index(y + 3), head), (z_index(z + 1), head), (z_index(z + 7), head)]
+    partners = [on_chip(t) for t in range(1, 4)] + [(ctx, sibling), (up_row, head), (down_row, head)] + rings
     barrier = pltpu.get_barrier_semaphore()
     for c, h in partners:
         pl.semaphore_signal(barrier, inc=1, device_id=(c, h), device_id_type=MESH)
@@ -105,50 +108,89 @@
         return kw.at[pl.ds(pl.multiple_of(slot * 128 + h * 32, 32), 32)]
 
     def kz(d):
-        to = (ctx + (2 * d if d < 4 else 7)) % 64
-        return rcopy(krows(7, head), krows(7 - 2 * d if d < 4 else 0, head), kz_s.at[d], kz_r.at[d], to, head)
-
-    def kfwd(d, t):
-        m, a2, h2 = mate(t)
-        return rcopy(
-            krows(7 - 2 * d, head), krows(7 - (2 * d + a2 - a), head),
-            kr_s.at[d, t], kr_r.at[d, me], row * 2 + a2, h2,
-        )
-
-    def kgot(d, t):
-        m, a2, h2 = mate(t)
-        ref = krows(7 - (2 * d + a - a2), h2)
-        return rcopy(ref, ref, kr_s.at[d, t], kr_r.at[d, m], row * 2 + a2, h2)
-
-    def kfirst(h2):
-        return rcopy(krows(7, head), krows(6, head), kr_s.at[0, h2], kr_r.at[0, head], row * 2 + 1, h2)
-
-    def kfirst_got(h2):
-        return rcopy(krows(6, h2), krows(6, h2), kr_s.at[0, h2], kr_r.at[0, h2], row * 2, h2)
-
-    def klast(t):
-        return rcopy(krows(0, head), krows(0, head), kr_s.at[4, t], kr_r.at[4, head], row * 2, (head + t) % 4)
-
-    def klast_got(t):
-        h2 = (head + t) % 4
-        return rcopy(krows(0, h2), krows(0, h2), kr_s.at[4, t], kr_r.at[4, h2], row * 2, h2)
-
-    for d in (1, 2, 3):
-        kz(d).start()
-
-    @pl.when(a == 1)
-    def _():
-        kz(4).start()
+        src = krows(9 - 2 * d, head)
+        dst = krows(7 - 2 * d, head) if d < 4 else k4
+        return rcopy(src, dst, kz_s.at[d], kz_r.at[d], up_row, head)
+
+    def kz_got(d):
+        ref = krows(7 - 2 * d, head) if d < 4 else k4
+        return rcopy(ref, ref, kz_s.at[d], kz_r.at[d], down_row, head)
+
+    def kx(d, t):
+        x2, a2, hi2 = chip_at(t)
+        src = krows(7 - 2 * d, head) if d < 4 else k4
+        dst = krows(7 - (2 * d + a2 - a), head) if d < 4 else krows(0, head)
+        return rcopy(src, dst, kx_s.at[d, t], kx_r.at[d, chip], row * 2 + a2, hi2 * 2 + core)
+
+    def kpiece(d, x2, cc):
+        slot = 7 - (2 * d + a - x2 % 2) if d < 4 else 0
+        return krows(slot, (x2 // 2) * 2 + cc)
+
+    def kx_got(d, t):
+        x2, a2, hi2 = chip_at(t)
+        ref = kpiece(d, x2, core)
+        return rcopy(ref, ref, kx_s.at[d, t], kx_r.at[d, x2], row * 2 + a2, hi2 * 2 + core)
+
+    def kc(d, t):
+        x2, a2, hi2 = chip_at(t)
+        ref = kpiece(d, x2, core)
+        return rcopy(ref, ref, kc_s.at[d, x2], kc_r.at[d, x2], ctx, sibling)
+
+    def kc_got(d, t):
+        x2, a2, hi2 = chip_at(t)
+        ref = kpiece(d, x2, 1 - core)
+        return rcopy(ref, ref, kc_s.at[d, x2], kc_r.at[d, x2], ctx, sibling)
+
+    def arrive(d):
+        if d < 4:
+            kz_got(d).wait_recv()
+            if d < 3:
+                kz(d + 1).start()
+            else:
+                @pl.when(a == 1)
+                def _():
+                    kz(4).start()
+            for t in (1, 3, 2):
+                kx(d, t).start()
+            kc(d, 0).start()
+        else:
+            @pl.when(a == 1)
+            def _():
+                kz_got(4).wait_recv()
+                for t in (1, 3):
+                    kx(4, t).start()
+
+    def pass_on(d):
+        if d in (1, 2, 3):
+            for t in (1, 3, 2):
+                kx_got(d, t).wait_recv()
+                kc(d, t).start()
+        else:
+            @pl.when(a == (1 if d == 0 else 0))
+            def _():
+                for t in (1, 3):
+                    kx_got(d, t).wait_recv()
+                    kc(d, t).start()
+
+    def complete(d):
+        if d in (1, 2, 3):
+            for t in range(4):
+                kc_got(d, t).wait_recv()
+        else:
+            @pl.when(a == (1 if d == 0 else 0))
+            def _():
+                for t in (1, 3):
+                    kc_got(d, t).wait_recv()
+
+    kz(1).start()
 
     @pl.when(a == 0)
     def _():
-        for h2 in range(4):
-            kfirst(h2).start()
-
-    def forward(d):
-        kz(d).wait_recv()
-        for t in range(1, 8):
-            kfwd(d, t).start()
+        for t in (1, 3):
+            kx(0, t).start()
+
+    for c, h in rings:
+        pl.semaphore_signal(ring_sem.at[0], inc=1, device_id=(c, h), device_id_type=MESH)
 
     def vup_in(i, c):
         v = vup_raw[pl.ds(i * 8, 8)].astype(F32).reshape(128, 128)
@@ -180,14 +222,23 @@
         return c
 
     in_copies[1].wait()
-    lax.fori_loop(0, 64, vup_in, 0)
+    lax.fori_loop(0, 32, vup_in, 0)
+    arrive(1)
+    lax.fori_loop(32, 64, vup_in, 0)
+    pass_on(0)
     in_copies[2].wait()
     lax.fori_loop(0, 16, cot_in, 0)
-    forward(1)
-    lax.fori_loop(0, 8, head_up, 0)
-    forward(2)
-    lax.fori_loop(8, 16, head_up, 0)
-    forward(3)
+    arrive(2)
+    pass_on(1)
+    lax.fori_loop(0, 4, head_up, 0)
+    arrive(3)
+    pass_on(2)
+    lax.fori_loop(4, 8, head_up, 0)
+    arrive(4)
+    pass_on(3)
+    lax.fori_loop(8, 12, head_up, 0)
+    pass_on(4)
+    lax.fori_loop(12, 16, head_up, 0)
 
     def cx_copy(hg):
         return rcopy(
@@ -214,21 +265,7 @@
         ref = coty.at[r, pl.ds(pl.multiple_of(128 * y2, 128), 128)]
         return rcopy(ref, ref, cy_s.at[r, t], cy_r.at[r, y2], y2 * 16 + ctx % 16, head)
 
-    for hg in range(4):
-        cx_copy(hg).start()
-        cotx[hg, pl.ds(pl.multiple_of(128 * a, 128), 128), :] = cot_h[4 * hg + a]
-    for r in range(2):
-        for t in range(1, 4):
-            cy_copy(r, t).start()
-        coty[r, pl.ds(pl.multiple_of(128 * y, 128), 128), :] = cot_h[y_head(r, y)]
-
     lax.fori_loop(0, 16, head_q, 0)
-
-    @pl.when(a == 0)
-    def _():
-        kz(4).wait_recv()
-        for t in range(1, 4):
-            klast(t).start()
 
     for w in range(8):
         back = 896 - w * 128 + lane - sub
@@ -252,31 +289,30 @@
             if w < 7:
                 k_t[:, w * 128:(w + 1) * 128] = kw[w * 128:(w + 1) * 128, :].T
 
-    def arrived(d):
-        for t in range(1, 8):
-            kgot(d, t).wait_recv()
-
-    @pl.when(a == 1)
-    def _():
-        for h2 in range(4):
-            kfirst_got(h2).wait_recv()
-
-    arrived(1)
+    complete(0)
+    complete(1)
     score_group(3)
-    arrived(2)
+    complete(2)
+    pl.semaphore_wait(ring_sem.at[0], 4)
+    for c, h in rings[2:]:
+        pl.semaphore_signal(ring_sem.at[1], inc=1, device_id=(c, h), device_id_type=MESH)
     score_group(2)
-    arrived(3)
+    complete(3)
+    pl.semaphore_wait(ring_sem.at[1], 2)
+    for c, h in rings[2:]:
+        pl.semaphore_signal(ring_sem.at[2], inc=1, device_id=(c, h), device_id_type=MESH)
     score_group(1)
-
-    @pl.when(a == 0)
-    def _():
-        for t in range(1, 4):
-            klast_got(t).wait_recv()
-
+    complete(4)
     score_group(0)
-
-    def y_index(y2):
-        return y2 * 16 + ctx % 16
+    pl.semaphore_wait(ring_sem.at[2], 2)
+
+    for hg in range(4):
+        cx_copy(hg).start()
+        cotx[hg, pl.ds(pl.multiple_of(128 * a, 128), 128), :] = cot_h[4 * hg + a]
+    for r in range(2):
+        for t in range(1, 4):
+            cy_copy(r, t).start()
+        coty[r, pl.ds(pl.multiple_of(128 * y, 128), 128), :] = cot_h[y_head(r, y)]
 
     def ox_copy(hg):
         cols = pl.ds(pl.multiple_of(128 * a, 128), 128)
@@ -475,35 +511,31 @@
     score_grads(3)
     fourth(0)
 
-    def quarter(slot, j):
-        return dks.at[slot, pl.ds(pl.multiple_of(144 * j, 16), 144)]
-
-    def dr_copy(d, t):
-        m, a2, h2 = mate(t)
+    def half_rows(cc):
+        return pl.ds(pl.multiple_of(288 * cc, 16), 288)
+
+    def quarter_rows(hi2):
+        return pl.ds(pl.multiple_of(144 * hi2, 16), 144)
+
+    def dc_copy(g):
+        return rcopy(dks.at[pl.ds(2 * g, 2), half_rows(1 - core)], dcore.at[g], dc_s.at[g], dc_r.at[g], ctx, sibling)
+
+    def dx_copy(d, t):
+        x2, a2, hi2 = chip_at(t)
+        slot = 7 - (2 * d + a - a2) if d < 4 else 0
         return rcopy(
-            quarter(7 - (2 * d + a - a2), h2), drow.at[d, me], dr_s.at[d, t], dr_r.at[d, me], row * 2 + a2, h2
+            csb.at[slot, quarter_rows(hi2)], drow.at[d, chip], dx_s.at[d, t], dx_r.at[d, chip],
+            row * 2 + a2, hi2 * 2 + core,
         )
 
-    def dr_got(d, t):
-        m, a2, h2 = mate(t)
-        return rcopy(drow.at[d, m], drow.at[d, m], dr_s.at[d, t], dr_r.at[d, m], row * 2 + a2, h2)
-
-    def dr_last(h2):
-        return rcopy(quarter(0, h2), drow.at[4, head], dr_s.at[4, h2], dr_r.at[4, head], row * 2 + 1, h2)
-
-    def dr_last_got(h2):
-        return rcopy(drow.at[4, h2], drow.at[4, h2], dr_s.at[4, h2], dr_r.at[4, h2], row * 2, h2)
+    def dx_got(d, t):
+        x2, a2, hi2 = chip_at(t)
+        return rcopy(
+            drow.at[d, x2], drow.at[d, x2], dx_s.at[d, t], dx_r.at[d, x2], row * 2 + a2, hi2 * 2 + core
+        )
 
     def dz_copy(d):
-        return rcopy(zsend.at[d], zrecv.at[d], dz_s.at[d], dz_r.at[d], (ctx + 64 - 2 * d) % 64, head)
-
-    def same_row(t):
-        m, a2, h2 = mate(t)
-        return a2 <= a
-
-    def same_row_got(t):
-        m, a2, h2 = mate(t)
-        return a2 >= a
+        return rcopy(zsend.at[d], zrecv.at[d], dz_s.at[d], dz_r.at[d], down_row, head)
 
     def key_grads(g):
         rows = slice(g * 256, g * 256 + 256)
@@ -511,59 +543,74 @@
         v = dot_nt(do_t[...], p_buf[rows, :])
         for i in range(2):
             part = slice(128 * i, 128 * i + 128)
-            dks[2 * g + i, :512, :] = (x[:512, part] + v[:, part]).astype(BF16)
-            dks[2 * g + i, 512:, :] = x[512:, part].astype(BF16)
+            dks[2 * g + i, :512, :] = x[:512, part] + v[:, part]
+            dks[2 * g + i, 512:, :] = x[512:, part]
+        dc_copy(g).start()
+
+    def chip_sum(g):
+        dc_copy(g).wait_recv()
+        for i in range(2):
+            total = dks[2 * g + i, half_rows(core), :] + dcore[g, i]
+            csf[2 * g + i] = total
+            csb[2 * g + i] = total.astype(BF16)
+
+        @pl.when(a == 1)
+        def _():
+            for t in (1, 3, 2):
+                dx_copy(3 - g, t).start()
+
+        @pl.when(a == 0)
+        def _():
+            for t in (1, 3, 2) if g > 0 else (1, 3):
+                dx_copy(4 - g, t).start()
+            if g == 3:
+                dx_copy(0, 2).start()
+
+    def own_part(d):
+        return csf[7 - 2 * d, quarter_rows(head // 2), :]
 
     def row_sum(d):
-        for t in range(1, 8):
-            dr_got(d, t).wait_recv()
-        total = quarter(7 - 2 * d, head)[...].astype(F32)
-        for t in range(1, 8):
-            total = total + drow[d, (me + t) % 8].astype(F32)
+        total = own_part(d)
+        for t in range(1, 4):
+            dx_got(d, t).wait_recv()
+        for t in range(1, 4):
+            total = total + drow[d, (chip + t) % 4].astype(F32)
+        if d < 3:
+            dz_copy(d + 1).wait_recv()
+            total = total + zrecv[d + 1]
+        else:
+            @pl.when(a == 1)
+            def _():
+                dz_copy(4).wait_recv()
+            total = total + zrecv[4]
         zsend[d] = total
         dz_copy(d).start()
-
-    @pl.when(a == 1)
-    def _():
-        drow[0, 0:4] = jnp.zeros((4, 144, 128), BF16)
 
     @pl.when(a == 0)
     def _():
         zrecv[4] = jnp.zeros((144, 128), F32)
 
-    key_grads(0)
-
-    @pl.when(a == 0)
-    def _():
-        for h2 in range(4):
-            dr_last(h2).start()
-
-    key_grads(1)
-    for t in range(1, 8):
-        dr_copy(3, t).start()
-    key_grads(2)
-    for t in range(1, 8):
-        dr_copy(2, t).start()
-    row_sum(3)
-
     @pl.when(a == 1)
     def _():
-        for h2 in range(4):
-            dr_last_got(h2).wait_recv()
-        total = drow[4, 0].astype(F32)
-        for h2 in range(1, 4):
-            total = total + drow[4, h2].astype(F32)
-        zsend[4] = total
+        drow[0, 0] = jnp.zeros((144, 128), BF16)
+        drow[0, 2] = jnp.zeros((144, 128), BF16)
+
+    key_grads(0)
+    key_grads(1)
+    chip_sum(0)
+    key_grads(2)
+    chip_sum(1)
+
+    @pl.when(a == 1)
+    def _():
+        for t in (1, 3):
+            dx_got(4, t).wait_recv()
+        zsend[4] = drow[4, 0].astype(F32) + drow[4, 2].astype(F32)
         dz_copy(4).start()
 
     key_grads(3)
-    for t in range(1, 8):
-        dr_copy(1, t).start()
-    for t in range(1, 8):
-        @pl.when(same_row(t))
-        def _():
-            dr_copy(0, t).start()
-    row_sum(2)
+    chip_sum(2)
+    row_sum(3)
 
     def gq_copy(h):
         return pltpu.make_async_copy(gq.at[h], gq_hbm.at[h], gq_sem.at[h])
@@ -580,34 +627,32 @@
             gq_copy(h).start()
         return c
 
-    lax.fori_loop(0, 2, dq, 0)
+    lax.fori_loop(0, 1, dq, 0)
+    chip_sum(3)
+    row_sum(2)
+    lax.fori_loop(1, 2, dq, 0)
+    fourth(1)
     row_sum(1)
-
-    fourth(1)
+    lax.fori_loop(2, 3, dq, 0)
     fifth(0)
-    lax.fori_loop(2, 4, dq, 0)
-
-    for t in range(1, 8):
-        @pl.when(same_row_got(t))
+
+    total = own_part(0)
+    for t in range(1, 4):
+        x2, a2, hi2 = chip_at(t)
+
+        @pl.when(a2 >= a)
         def _():
-            dr_got(0, t).wait_recv()
-    total = quarter(7, head)[...].astype(F32)
-    for t in range(1, 8):
-        total = total + drow[0, (me + t) % 8].astype(F32)
-    for d in (1, 2, 3):
-        dz_copy(d).wait_recv()
-
-    @pl.when(a == 1)
-    def _():
-        dz_copy(4).wait_recv()
-
-    for d in (1, 2, 3, 4):
-        total = total + zrecv[d]
-    roped = head == 3
+            dx_got(0, t).wait_recv()
+    for t in range(1, 4):
+        total = total + drow[0, (chip + t) % 4].astype(F32)
+    dz_copy(1).wait_recv()
+    total = total + zrecv[1]
+    quarter = 2 * core + head // 2
+    roped = quarter == 3
     cosine = jnp.where(roped, tab[0], 1.0)
     sine = jnp.where(roped, tab[1], 0.0)
     lower, upper = total[80:112], total[112:144]
-    own_quarter = glt.at[pl.ds(pl.multiple_of(144 * head, 16), 144)]
+    own_quarter = glt.at[pl.ds(pl.multiple_of(144 * quarter, 16), 144)]
     own_quarter[...] = jnp.concatenate(
         [total[:80], lower * cosine + upper * sine, upper * cosine - lower * sine], axis=0
     ).astype(BF16)
@@ -617,11 +662,12 @@
 
     def gl_got(t):
         h2 = (head + t) % 4
-        ref = glt.at[pl.ds(pl.multiple_of(144 * h2, 16), 144)]
+        ref = glt.at[pl.ds(pl.multiple_of(144 * (2 * (h2 % 2) + h2 // 2), 16), 144)]
         return rcopy(ref, ref, gl_s.at[t], gl_r.at[h2], ctx, h2)
 
     for t in range(1, 4):
         gl_copy(t).start()
+    lax.fori_loop(3, 4, dq, 0)
     fifth(1)
     outs.append(pltpu.make_async_copy(gv, gv_hbm, out_sem.at[1]))
     outs[-1].start()
@@ -633,28 +679,31 @@
 
     for d in (1, 2, 3):
         kz(d).wait_send()
-        for t in range(1, 8):
-            kfwd(d, t).wait_send()
-            dr_copy(d, t).wait_send()
+        for t in range(4):
+            kc(d, t).wait_send()
+        for t in range(1, 4):
+            kx(d, t).wait_send()
+            dx_copy(d, t).wait_send()
         dz_copy(d).wait_send()
+    dx_copy(0, 2).wait_send()
+    for g in range(4):
+        dc_copy(g).wait_send()
 
     @pl.when(a == 1)
     def _():
         kz(4).wait_send()
         dz_copy(4).wait_send()
+        for t in (1, 3):
+            kx(4, t).wait_send()
+            kc(0, t).wait_send()
+            dx_copy(0, t).wait_send()
 
     @pl.when(a == 0)
     def _():
-        for h2 in range(4):
-            kfirst(h2).wait_send()
-            dr_last(h2).wait_send()
-        for t in range(1, 4):
-            klast(t).wait_send()
-
-    for t in range(1, 8):
-        @pl.when(same_row(t))
-        def _():
-            dr_copy(0, t).wait_send()
+        for t in (1, 3):
+            kx(0, t).wait_send()
+            kc(4, t).wait_send()
+            dx_copy(4, t).wait_send()
 
     for t in range(1, 4):
         gl_copy(t).wait_send()
@@ -680,6 +729,15 @@
         c.wait()
     for h in range(16):
         gq_copy(h).wait()
+
+
+def handed_on(attn, gq, gl, gv, attn_out, gq_out, gl_out, gv_out, sem):
+    pairs = [(gq.at[h], gq_out.at[h]) for h in range(16)] + [(attn, attn_out), (gl, gl_out), (gv, gv_out)]
+    copies = [pltpu.make_async_copy(src, dst, sem.at[i]) for i, (src, dst) in enumerate(pairs)]
+    for c in copies:
+        c.start()
+    for c in copies:
+        c.wait()
 
 
 def body(queries, latent_kv, positions, value_up, cotangent):
@@ -702,20 +760,22 @@
             vmem((576, 2048), BF16), vmem((512, 2048), BF16),
             vmem((16, 512, 128), BF16), vmem((16, 128, 512), BF16), vmem((16, 128, 128), BF16),
             vmem((1024, 2048), BF16), vmem((1024, 2048), BF16), vmem((1024, 128), F32), vmem((16, 8, 128), F32),
-            vmem((2048, 128), F32), vmem((1024, 576), BF16), vmem((576, 1024), BF16),
+            vmem((2048, 128), F32), vmem((1024, 576), BF16), vmem((576, 1024), BF16), vmem((32, 576), BF16),
             vmem((16, 512, 128), BF16), vmem((4, 512, 256), BF16), vmem((2, 512, 512), BF16),
             vmem((4, 256, 128), BF16), vmem((2, 512, 128), BF16), vmem((4, 512, 128), F32), vmem((4, 512, 128), BF16),
             vmem((4, 3, 128, 128), BF16), vmem((2, 2, 256, 128), F32), vmem((2, 2, 256, 128), BF16),
             vmem((2, 256, 128), BF16), vmem((2, 8, 64, 128), F32), vmem((2, 7, 64, 128), F32),
             vmem((2, 16, 128), F32), vmem((2, 16, 128), F32), vmem((2, 32, 128), F32), vmem((2, 3, 8, 128), F32),
             vmem((128, 128), F32),
-            vmem((8, 576, 128), BF16), vmem((5, 8, 144, 128), BF16), vmem((5, 144, 128), F32),
+            vmem((8, 576, 128), F32), vmem((4, 2, 288, 128), F32), vmem((8, 288, 128), F32), vmem((8, 288, 128), BF16),
+            vmem((5, 4, 144, 128), BF16), vmem((5, 144, 128), F32),
             vmem((5, 144, 128), F32), vmem((576, 128), BF16),
-            dma((3,)), dma((16,)), dma((3,)), dma((16,)), dma((5,)), dma((5,)), dma((5, 8)), dma((5, 8)),
+            dma((3,)), dma((16,)), dma((3,)), dma((16,)), pltpu.SemaphoreType.REGULAR((3,)),
+            dma((5,)), dma((5,)), dma((5, 4)), dma((5, 4)), dma((5, 4)), dma((5, 4)),
             dma((4,)), dma((4,)), dma((2, 4)), dma((2, 4)), dma((4,)), dma((4,)), dma((4, 2)), dma((2, 4)),
             dma((4, 3)), dma((4, 3)), dma((2,)), dma((2,)), dma((2, 7)), dma((2, 7)), dma((2,)), dma((2,)),
             dma((2, 3)), dma((2, 3)),
-            dma((5, 8)), dma((5, 8)), dma((5,)), dma((5,)), dma((4,)), dma((4,)),
+            dma((4,)), dma((4,)), dma((5, 4)), dma((5, 4)), dma((5,)), dma((5,)), dma((4,)), dma((4,)),
         ],
         compiler_params=pltpu.CompilerParams(
             collective_id=0, has_side_effects=True, vmem_limit_bytes=64 * 2**20 - 2**16
@@ -723,6 +783,13 @@
     )(
         jnp.transpose(queries, (1, 2, 0)), latent_kv.T, positions.reshape(1, 128), value_up, cotangent
     )
+    attn, gq, gl, gv = pl.pallas_call(
+        handed_on,
+        out_shape=tuple(jax.ShapeDtypeStruct(x.shape, x.dtype) for x in (attn, gq, gl, gv)),
+        in_specs=[anywhere] * 4,
+        out_specs=(anywhere,) * 4,
+        scratch_shapes=[dma((19,))],
+    )(attn, gq, gl, gv)
     return attn, jnp.transpose(gq, (2, 0, 1)), gl.T, gv.reshape(8, 16, 128)
 
 

time: 103 us -> 190 us (1.84)
  the two profiles are of different devices: /device:TPU:27 before, /device:TPU:2 now
where the time goes in v4:
time: 190 us; the launch traced here: 186 us
  Pallas kernels  186 us (98%)
    pallas_call x1, Pallas kernels, body(): pl.pallas_call(handed_on, out_shape=tuple((jax.ShapeDtypeStruct(x.shape,...  95.1 us
    pallas_call x1, Pallas kernels, body(): pl.pallas_call(kernel, out_shape=(jax.ShapeDtypeStruct((128, 16, 128), BF...  90.5 us

profile of v4, /device:TPU:2, one launch (start us, length us, event | category | flops | bytes accessed | tf_op | source)
XLA Modules:
  0.0 186.4 jit_solution(16389838782858481247)
XLA Ops:
  0.6 90.5 %shard_map.84 = (bf16[128,16,128]{2,1,0:T(8,128)(2,1)}, bf16[16,576,128]{2,1,0:T(8,128)(2,1)}, bf16[576,128]{1,0:T(8,128)(2,1)}, f32[128,128]{1,0:T(8,128)}) custom-call(bf16[16,576,128]{2,1,0:T(8,128)(2,1)} %bitcast.6, bf16[576,128]{1,0:T(8,128)(2,1)} %bitcast.7, s32[1,128]{1,0:T(1,128)} %bitcast.8, bf16[512,16,128]{2,1,0:T(8,128)(2,1)} %vup_hbm.1, ...), custom_call_target="tpu_custom_call" | custom-call | tf_op jit(solution)/shard_map/pallas_call | solution.py:746
  91.1 95.1 %shard_map.85 = (bf16[128,16,128]{2,1,0:T(8,128)(2,1)}, bf16[16,576,128]{2,1,0:T(8,128)(2,1)}, bf16[576,128]{1,0:T(8,128)(2,1)}, f32[128,128]{1,0:T(8,128)}) custom-call(bf16[128,16,128]{2,1,0:T(8,128)(2,1)} %get-tuple-element.12.attn, bf16[16,576,128]{2,1,0:T(8,128)(2,1)} %get-tuple-element.13.gq, bf16[576,128]{1,0:T(8,128)(2,1)} %get-tuple-element.14.gl, ...), custom_call_target="tpu_custom_call" | custom-call | tf_op jit(solution)/shard_map/pallas_call | solution.py:786

commit v5 on v4

--- a/solution.py
+++ b/solution.py
@@ -221,25 +221,6 @@
         q_t[544:576, cols] = (upper * tab[0] + lower * tab[1]).astype(BF16)
         return c
 
-    in_copies[1].wait()
-    lax.fori_loop(0, 32, vup_in, 0)
-    arrive(1)
-    lax.fori_loop(32, 64, vup_in, 0)
-    pass_on(0)
-    in_copies[2].wait()
-    lax.fori_loop(0, 16, cot_in, 0)
-    arrive(2)
-    pass_on(1)
-    lax.fori_loop(0, 4, head_up, 0)
-    arrive(3)
-    pass_on(2)
-    lax.fori_loop(4, 8, head_up, 0)
-    arrive(4)
-    pass_on(3)
-    lax.fori_loop(8, 12, head_up, 0)
-    pass_on(4)
-    lax.fori_loop(12, 16, head_up, 0)
-
     def cx_copy(hg):
         return rcopy(
             cot_h.at[4 * hg + 1 - a], cotx.at[hg, pl.ds(pl.multiple_of(128 * a, 128), 128)],
@@ -265,17 +246,11 @@
         ref = coty.at[r, pl.ds(pl.multiple_of(128 * y2, 128), 128)]
         return rcopy(ref, ref, cy_s.at[r, t], cy_r.at[r, y2], y2 * 16 + ctx % 16, head)
 
-    lax.fori_loop(0, 16, head_q, 0)
-
-    for w in range(8):
-        back = 896 - w * 128 + lane - sub
-        bias[w * 128:(w + 1) * 128, :] = jnp.where((back >= 0) & (back <= pos_ref[...]), 0.0, -jnp.inf)
-
     def score_group(g):
         rows = slice(g * 256, g * 256 + 256)
 
         def qk(r, c):
-            s = dot(kw[rows, :], q_t[:, pl.ds(pl.multiple_of(r * 512, 512), 512)])
+            s = dot(kw[rows, :], q_t[:, r * 512:r * 512 + 512])
             for j in range(4):
                 h = r * 4 + j
                 x = s[:, j * 128:(j + 1) * 128] * (SCALE * LOG2E) + bias[rows, :]
@@ -284,19 +259,40 @@
                 peak[h] = top if g == 3 else jnp.maximum(peak[h], top)
             return c
 
-        lax.fori_loop(0, 4, qk, 0)
+        for r in range(4):
+            qk(r, 0)
         for w in (2 * g, 2 * g + 1):
             if w < 7:
                 k_t[:, w * 128:(w + 1) * 128] = kw[w * 128:(w + 1) * 128, :].T
 
+    in_copies[1].wait()
+    lax.fori_loop(0, 64, vup_in, 0)
+    arrive(1)
+    pass_on(0)
+    in_copies[2].wait()
+    lax.fori_loop(0, 16, cot_in, 0)
+    lax.fori_loop(0, 6, head_up, 0)
+    arrive(2)
+    pass_on(1)
+    lax.fori_loop(6, 12, head_up, 0)
+    arrive(3)
+    pass_on(2)
+    lax.fori_loop(0, 16, head_q, 0)
+    for w in range(8):
+        back = 896 - w * 128 + lane - sub
+        bias[w * 128:(w + 1) * 128, :] = jnp.where((back >= 0) & (back <= pos_ref[...]), 0.0, -jnp.inf)
+    arrive(4)
+    lax.fori_loop(12, 16, head_up, 0)
     complete(0)
     complete(1)
     score_group(3)
+    pass_on(3)
     complete(2)
     pl.semaphore_wait(ring_sem.at[0], 4)
     for c, h in rings[2:]:
         pl.semaphore_signal(ring_sem.at[1], inc=1, device_id=(c, h), device_id_type=MESH)
     score_group(2)
+    pass_on(4)
     complete(3)
     pl.semaphore_wait(ring_sem.at[1], 2)
     for c, h in rings[2:]:
@@ -422,35 +418,24 @@
             gv[pl.ds(4 * (2 * r + y2 // 2) + 2 + y2 % 2, 8, stride=16), :] = rows
 
     def folded(x):
-        return jnp.sum(x.reshape(16, 8, 128), axis=0)
-
-    def block(i):
-        return pl.ds(pl.multiple_of(i * 128, 128), 128)
-
-    def softmax(h, c):
-        cols = pl.ds(pl.multiple_of(h * 128, 128), 128)
-        top = jnp.max(peak[h], axis=0, keepdims=True)
-
-        def exps(i, mass):
-            e = jnp.exp2(s_buf[h, block(i), :] - top)
-            s_buf[h, block(i), :] = e
-            return mass + folded(e)
-
-        mass = lax.fori_loop(0, 8, exps, jnp.zeros((8, 128), F32), unroll=2)
-        inverse = 1.0 / jnp.sum(mass, axis=0, keepdims=True)
-
-        def probs(i, c2):
-            p_buf[block(i), cols] = (s_buf[h, block(i), :] * inverse).astype(BF16)
-            return c2
-
-        lax.fori_loop(0, 8, probs, 0, unroll=2)
-        return c
-
+        return jnp.sum(jnp.sum(x.reshape(128, 8, 128), axis=0), axis=0, keepdims=True)
+
+    def softmax(hg):
+        for h in range(4 * hg, 4 * hg + 4):
+            cols = slice(128 * h, 128 * h + 128)
+            e = jnp.exp2(s_buf[h] - jnp.max(peak[h], axis=0, keepdims=True))
+            s_buf[h] = e
+            p_buf[:, cols] = (s_buf[h] * (1.0 / folded(e))).astype(BF16)
+
+    softmax(0)
     for hg in range(4):
-        lax.fori_loop(4 * hg, 4 * hg + 4, softmax, 0)
         o = dot(k_t[:512, :], p_buf[:, hg * 512:hg * 512 + 512]).astype(BF16)
         for j in range(4):
             o_buf[4 * hg + j] = o[:, j * 128:(j + 1) * 128]
+        if hg < 3:
+            softmax(hg + 1)
+        for j in range(4):
+            ao[pl.ds(4 * hg + j, 128, stride=16), :] = dot(vup_t[4 * hg + j], o[:, j * 128:(j + 1) * 128]).T
         ox_copy(hg).start()
         ox[hg, :, pl.ds(pl.multiple_of(128 * a, 128), 128)] = o_buf[4 * hg + a]
         for j in range(2):
@@ -461,13 +446,6 @@
             @pl.when(y == 2 * (hg % 2) + j)
             def _():
                 oy[hg // 2, :, pl.ds(pl.multiple_of(128 * y, 128), 128)] = o_buf[4 * hg + 2 + j]
-        for j in range(4):
-            h = hg * 4 + j
-            ao[pl.ds(h, 128, stride=16), :] = dot(vup_t[h], o[:, j * 128:(j + 1) * 128]).T
-        if hg >= 1:
-            x_second(hg - 1)
-        if hg == 2:
-            y_second(0)
 
     def attn16(i, c):
         cot_raw[pl.ds(i * 8, 8)] = ao[pl.ds(i * 128, 128), :].reshape(8, 16, 128).astype(BF16)
@@ -478,38 +456,15 @@
     outs[0].start()
 
     def score_grads(hg):
-        dp_buf[...] = dot(kw[:, :512], do_t[:, hg * 512:hg * 512 + 512]) * SCALE
-
-        def one_head(j, c):
-            h = hg * 4 + j
-            cols = pl.ds(pl.multiple_of(h * 128, 128), 128)
-            dp_cols = pl.ds(pl.multiple_of(j * 128, 128), 128)
-
-            def deltas(i, delta):
-                return delta + folded(p_buf[block(i), cols].astype(F32) * dp_buf[block(i), dp_cols])
-
-            delta = lax.fori_loop(0, 8, deltas, jnp.zeros((8, 128), F32), unroll=2)
-            delta = jnp.sum(delta, axis=0, keepdims=True)
-
-            def grads(i, c2):
-                p = p_buf[block(i), cols].astype(F32)
-                ds_buf[block(i), cols] = (p * (dp_buf[block(i), dp_cols] - delta)).astype(BF16)
-                return c2
-
-            lax.fori_loop(0, 8, grads, 0, unroll=2)
-            return c
-
-        lax.fori_loop(0, 4, one_head, 0)
-
-    score_grads(0)
-    x_second(3)
-    y_second(1)
-    third(0)
-    score_grads(1)
-    score_grads(2)
-    third(1)
-    score_grads(3)
-    fourth(0)
+        for j in range(4):
+            cols = slice((4 * hg + j) * 128, (4 * hg + j + 1) * 128)
+            if j % 2 == 0:
+                two = dot(kw[:, :512], do_t[:, hg * 512 + j * 128:hg * 512 + j * 128 + 256]) * SCALE
+            dp = two[:, (j % 2) * 128:(j % 2) * 128 + 128]
+            dp_buf[:, j * 128:(j + 1) * 128] = dp
+            delta = folded(p_buf[:, cols].astype(F32) * dp)
+            p = p_buf[:, cols].astype(F32)
+            ds_buf[:, cols] = (p * (dp_buf[:, j * 128:(j + 1) * 128] - delta)).astype(BF16)
 
     def half_rows(cc):
         return pl.ds(pl.multiple_of(288 * cc, 16), 288)
@@ -595,23 +550,6 @@
         drow[0, 0] = jnp.zeros((144, 128), BF16)
         drow[0, 2] = jnp.zeros((144, 128), BF16)
 
-    key_grads(0)
-    key_grads(1)
-    chip_sum(0)
-    key_grads(2)
-    chip_sum(1)
-
-    @pl.when(a == 1)
-    def _():
-        for t in (1, 3):
-            dx_got(4, t).wait_recv()
-        zsend[4] = drow[4, 0].astype(F32) + drow[4, 2].astype(F32)
-        dz_copy(4).start()
-
-    key_grads(3)
-    chip_sum(2)
-    row_sum(3)
-
     def gq_copy(h):
         return pltpu.make_async_copy(gq.at[h], gq_hbm.at[h], gq_sem.at[h])
 
@@ -627,14 +565,41 @@
             gq_copy(h).start()
         return c
 
+    score_grads(0)
+    score_grads(1)
+    x_second(0)
+    score_grads(2)
+    x_second(1)
+    y_second(0)
+    score_grads(3)
+    x_second(2)
+    key_grads(0)
+    key_grads(1)
+    chip_sum(0)
+    x_second(3)
+    y_second(1)
+    key_grads(2)
+    chip_sum(1)
+
+    @pl.when(a == 1)
+    def _():
+        for t in (1, 3):
+            dx_got(4, t).wait_recv()
+        zsend[4] = drow[4, 0].astype(F32) + drow[4, 2].astype(F32)
+        dz_copy(4).start()
+
+    third(0)
+    key_grads(3)
+    chip_sum(2)
     lax.fori_loop(0, 1, dq, 0)
+    row_sum(3)
     chip_sum(3)
+    lax.fori_loop(1, 2, dq, 0)
     row_sum(2)
-    lax.fori_loop(1, 2, dq, 0)
-    fourth(1)
+    third(1)
+    lax.fori_loop(2, 3, dq, 0)
     row_sum(1)
-    lax.fori_loop(2, 3, dq, 0)
-    fifth(0)
+    lax.fori_loop(3, 4, dq, 0)
 
     total = own_part(0)
     for t in range(1, 4):
@@ -667,7 +632,9 @@
 
     for t in range(1, 4):
         gl_copy(t).start()
-    lax.fori_loop(3, 4, dq, 0)
+    fourth(0)
+    fourth(1)
+    fifth(0)
     fifth(1)
     outs.append(pltpu.make_async_copy(gv, gv_hbm, out_sem.at[1]))
     outs[-1].start()
@@ -732,7 +699,7 @@
 
 
 def handed_on(attn, gq, gl, gv, attn_out, gq_out, gl_out, gv_out, sem):
-    pairs = [(gq.at[h], gq_out.at[h]) for h in range(16)] + [(attn, attn_out), (gl, gl_out), (gv, gv_out)]
+    pairs = [(gq, gq_out), (attn, attn_out), (gl, gl_out), (gv, gv_out)]
     copies = [pltpu.make_async_copy(src, dst, sem.at[i]) for i, (src, dst) in enumerate(pairs)]
     for c in copies:
         c.start()
@@ -786,9 +753,9 @@
     attn, gq, gl, gv = pl.pallas_call(
         handed_on,
         out_shape=tuple(jax.ShapeDtypeStruct(x.shape, x.dtype) for x in (attn, gq, gl, gv)),
-        in_specs=[anywhere] * 4,
+        in_specs=[pl.BlockSpec(memory_space=pltpu.VMEM)] * 4,
         out_specs=(anywhere,) * 4,
-        scratch_shapes=[dma((19,))],
+        scratch_shapes=[dma((4,))],
     )(attn, gq, gl, gv)
     return attn, jnp.transpose(gq, (2, 0, 1)), gl.T, gv.reshape(8, 16, 128)
 

time: 190 us -> 83.2 us (0.44); the launches traced: 186 us -> 82.3 us
  Pallas kernels: 186 us -> 81.5 us
    pallas_call x1, Pallas kernels: 95.1 us -> 3.44 us  [body(): pl.pallas_call(handed_on, out_shape=tuple((jax.ShapeDtypeStruct(x.shape,...]
    pallas_call x1, Pallas kernels: 90.5 us -> 78 us  [body(): pl.pallas_call(kernel, out_shape=(jax.ShapeDtypeStruct((128, 16, 128), BF...]
where the time goes in v5:
time: 83.2 us; the launch traced here: 82.3 us
  Pallas kernels  81.5 us (98%)
    pallas_call x1, Pallas kernels, body(): pl.pallas_call(kernel, out_shape=(jax.ShapeDtypeStruct((128, 16, 128), BF...  78 us
    pallas_call x1, Pallas kernels, body(): pl.pallas_call(handed_on, out_shape=tuple((jax.ShapeDtypeStruct(x.shape,...  3.44 us

profile of v5, /device:TPU:2, one launch (start us, length us, event | category | flops | bytes accessed | tf_op | source)
XLA Modules:
  0.0 82.3 jit_solution(12775116311981855582)
XLA Ops:
  0.6 78.0 %shard_map.84 = (bf16[128,16,128]{2,1,0:T(8,128)(2,1)}, bf16[16,576,128]{2,1,0:T(8,128)(2,1)}, bf16[576,128]{1,0:T(8,128)(2,1)}, f32[128,128]{1,0:T(8,128)}) custom-call(bf16[16,576,128]{2,1,0:T(8,128)(2,1)} %bitcast.6, bf16[576,128]{1,0:T(8,128)(2,1)} %bitcast.7, s32[1,128]{1,0:T(1,128)} %bitcast.8, bf16[512,16,128]{2,1,0:T(8,128)(2,1)} %vup_hbm.1, ...), custom_call_target="tpu_custom_call" | custom-call | tf_op jit(solution)/shard_map/pallas_call | solution.py:713
  78.7 3.4 %shard_map.85 = (bf16[128,16,128]{2,1,0:T(8,128)(2,1)}, bf16[16,576,128]{2,1,0:T(8,128)(2,1)}, bf16[576,128]{1,0:T(8,128)(2,1)}, f32[128,128]{1,0:T(8,128)}) custom-call(bf16[128,16,128]{2,1,0:T(8,128)(2,1)} %get-tuple-element.12.attn, bf16[16,576,128]{2,1,0:T(8,128)(2,1)} %get-tuple-element.13.gq, bf16[576,128]{1,0:T(8,128)(2,1)} %get-tuple-element.14.gl, ...), custom_call_target="tpu_custom_call" | custom-call | tf_op jit(solution)/shard_map/pallas_call | solution.py:753

commit v6 on v5

--- a/solution.py
+++ b/solution.py
@@ -265,34 +265,42 @@
             if w < 7:
                 k_t[:, w * 128:(w + 1) * 128] = kw[w * 128:(w + 1) * 128, :].T
 
+    arrive(1)
     in_copies[1].wait()
-    lax.fori_loop(0, 64, vup_in, 0)
-    arrive(1)
+    lax.fori_loop(0, 32, vup_in, 0)
+    arrive(2)
     pass_on(0)
+    lax.fori_loop(32, 64, vup_in, 0)
+    pass_on(1)
+    arrive(3)
     in_copies[2].wait()
     lax.fori_loop(0, 16, cot_in, 0)
-    lax.fori_loop(0, 6, head_up, 0)
-    arrive(2)
-    pass_on(1)
-    lax.fori_loop(6, 12, head_up, 0)
-    arrive(3)
+    lax.fori_loop(0, 4, head_up, 0)
     pass_on(2)
+    arrive(4)
+    lax.fori_loop(4, 10, head_up, 0)
+    pass_on(3)
+    lax.fori_loop(10, 16, head_up, 0)
+    pass_on(4)
     lax.fori_loop(0, 16, head_q, 0)
     for w in range(8):
         back = 896 - w * 128 + lane - sub
         bias[w * 128:(w + 1) * 128, :] = jnp.where((back >= 0) & (back <= pos_ref[...]), 0.0, -jnp.inf)
-    arrive(4)
-    lax.fori_loop(12, 16, head_up, 0)
     complete(0)
     complete(1)
     score_group(3)
-    pass_on(3)
     complete(2)
     pl.semaphore_wait(ring_sem.at[0], 4)
+    for hg in range(4):
+        cx_copy(hg).start()
+        cotx[hg, pl.ds(pl.multiple_of(128 * a, 128), 128), :] = cot_h[4 * hg + a]
+    for r in range(2):
+        for t in range(1, 4):
+            cy_copy(r, t).start()
+        coty[r, pl.ds(pl.multiple_of(128 * y, 128), 128), :] = cot_h[y_head(r, y)]
     for c, h in rings[2:]:
         pl.semaphore_signal(ring_sem.at[1], inc=1, device_id=(c, h), device_id_type=MESH)
     score_group(2)
-    pass_on(4)
     complete(3)
     pl.semaphore_wait(ring_sem.at[1], 2)
     for c, h in rings[2:]:
@@ -301,14 +309,6 @@
     complete(4)
     score_group(0)
     pl.semaphore_wait(ring_sem.at[2], 2)
-
-    for hg in range(4):
-        cx_copy(hg).start()
-        cotx[hg, pl.ds(pl.multiple_of(128 * a, 128), 128), :] = cot_h[4 * hg + a]
-    for r in range(2):
-        for t in range(1, 4):
-            cy_copy(r, t).start()
-        coty[r, pl.ds(pl.multiple_of(128 * y, 128), 128), :] = cot_h[y_head(r, y)]
 
     def ox_copy(hg):
         cols = pl.ds(pl.multiple_of(128 * a, 128), 128)
@@ -576,10 +576,11 @@
     key_grads(0)
     key_grads(1)
     chip_sum(0)
-    x_second(3)
-    y_second(1)
     key_grads(2)
     chip_sum(1)
+    key_grads(3)
+    x_second(3)
+    chip_sum(2)
 
     @pl.when(a == 1)
     def _():
@@ -588,17 +589,16 @@
         zsend[4] = drow[4, 0].astype(F32) + drow[4, 2].astype(F32)
         dz_copy(4).start()
 
+    lax.fori_loop(0, 1, dq, 0)
+    chip_sum(3)
+    row_sum(3)
+    y_second(1)
+    lax.fori_loop(1, 2, dq, 0)
     third(0)
-    key_grads(3)
-    chip_sum(2)
-    lax.fori_loop(0, 1, dq, 0)
-    row_sum(3)
-    chip_sum(3)
-    lax.fori_loop(1, 2, dq, 0)
     row_sum(2)
-    third(1)
     lax.fori_loop(2, 3, dq, 0)
     row_sum(1)
+    third(1)
     lax.fori_loop(3, 4, dq, 0)
 
     total = own_part(0)

time: 83.2 us -> 91.3 us (1.097)
  Pallas kernels: 81.5 us -> 90.3 us
    pallas_call x1, Pallas kernels: 78 us -> 86.9 us  [body(): pl.pallas_call(kernel, out_shape=(jax.ShapeDtypeStruct((128, 16, 128), BF...]
where the time goes in v6:
time: 91.3 us; the launch traced here: 91.2 us
  Pallas kernels  90.3 us (99%)
    pallas_call x1, Pallas kernels, body(): pl.pallas_call(kernel, out_shape=(jax.ShapeDtypeStruct((128, 16, 128), BF...  86.9 us
    pallas_call x1, Pallas kernels, body(): pl.pallas_call(handed_on, out_shape=tuple((jax.ShapeDtypeStruct(x.shape,...  3.44 us

profile of v6, /device:TPU:2, one launch (start us, length us, event | category | flops | bytes accessed | tf_op | source)
XLA Modules:
  0.0 91.2 jit_solution(1975587410320597968)
XLA Ops:
  0.6 86.9 %shard_map.84 = (bf16[128,16,128]{2,1,0:T(8,128)(2,1)}, bf16[16,576,128]{2,1,0:T(8,128)(2,1)}, bf16[576,128]{1,0:T(8,128)(2,1)}, f32[128,128]{1,0:T(8,128)}) custom-call(bf16[16,576,128]{2,1,0:T(8,128)(2,1)} %bitcast.6, bf16[576,128]{1,0:T(8,128)(2,1)} %bitcast.7, s32[1,128]{1,0:T(1,128)} %bitcast.8, bf16[512,16,128]{2,1,0:T(8,128)(2,1)} %vup_hbm.1, ...), custom_call_target="tpu_custom_call" | custom-call | tf_op jit(solution)/shard_map/pallas_call | solution.py:713
  87.5 3.4 %shard_map.85 = (bf16[128,16,128]{2,1,0:T(8,128)(2,1)}, bf16[16,576,128]{2,1,0:T(8,128)(2,1)}, bf16[576,128]{1,0:T(8,128)(2,1)}, f32[128,128]{1,0:T(8,128)}) custom-call(bf16[128,16,128]{2,1,0:T(8,128)(2,1)} %get-tuple-element.12.attn, bf16[16,576,128]{2,1,0:T(8,128)(2,1)} %get-tuple-element.13.gq, bf16[576,128]{1,0:T(8,128)(2,1)} %get-tuple-element.14.gl, ...), custom_call_target="tpu_custom_call" | custom-call | tf_op jit(solution)/shard_map/pallas_call | solution.py:753

commit v7 on v6

--- a/solution.py
+++ b/solution.py
@@ -279,25 +279,18 @@
     pass_on(2)
     arrive(4)
     lax.fori_loop(4, 10, head_up, 0)
-    pass_on(3)
     lax.fori_loop(10, 16, head_up, 0)
-    pass_on(4)
     lax.fori_loop(0, 16, head_q, 0)
     for w in range(8):
         back = 896 - w * 128 + lane - sub
         bias[w * 128:(w + 1) * 128, :] = jnp.where((back >= 0) & (back <= pos_ref[...]), 0.0, -jnp.inf)
     complete(0)
     complete(1)
+    pass_on(3)
     score_group(3)
+    pass_on(4)
     complete(2)
     pl.semaphore_wait(ring_sem.at[0], 4)
-    for hg in range(4):
-        cx_copy(hg).start()
-        cotx[hg, pl.ds(pl.multiple_of(128 * a, 128), 128), :] = cot_h[4 * hg + a]
-    for r in range(2):
-        for t in range(1, 4):
-            cy_copy(r, t).start()
-        coty[r, pl.ds(pl.multiple_of(128 * y, 128), 128), :] = cot_h[y_head(r, y)]
     for c, h in rings[2:]:
         pl.semaphore_signal(ring_sem.at[1], inc=1, device_id=(c, h), device_id_type=MESH)
     score_group(2)
@@ -309,6 +302,13 @@
     complete(4)
     score_group(0)
     pl.semaphore_wait(ring_sem.at[2], 2)
+    for hg in range(4):
+        cx_copy(hg).start()
+        cotx[hg, pl.ds(pl.multiple_of(128 * a, 128), 128), :] = cot_h[4 * hg + a]
+    for r in range(2):
+        for t in range(1, 4):
+            cy_copy(r, t).start()
+        coty[r, pl.ds(pl.multiple_of(128 * y, 128), 128), :] = cot_h[y_head(r, y)]
 
     def ox_copy(hg):
         cols = pl.ds(pl.multiple_of(128 * a, 128), 128)

time: 91.3 us -> 89.9 us (0.985)
  Pallas kernels: 90.3 us -> 89 us
    pallas_call x1, Pallas kernels: 86.9 us -> 85.5 us  [body(): pl.pallas_call(kernel, out_shape=(jax.ShapeDtypeStruct((128, 16, 128), BF...]
where the time goes in v7:
time: 89.9 us; the launch traced here: 89.8 us
  Pallas kernels  89 us (99%)
    pallas_call x1, Pallas kernels, body(): pl.pallas_call(kernel, out_shape=(jax.ShapeDtypeStruct((128, 16, 128), BF...  85.5 us
    pallas_call x1, Pallas kernels, body(): pl.pallas_call(handed_on, out_shape=tuple((jax.ShapeDtypeStruct(x.shape,...  3.44 us

profile of v7, /device:TPU:2, one launch (start us, length us, event | category | flops | bytes accessed | tf_op | source)
XLA Modules:
  0.0 89.8 jit_solution(18066007130738053565)
XLA Ops:
  0.6 85.5 %shard_map.84 = (bf16[128,16,128]{2,1,0:T(8,128)(2,1)}, bf16[16,576,128]{2,1,0:T(8,128)(2,1)}, bf16[576,128]{1,0:T(8,128)(2,1)}, f32[128,128]{1,0:T(8,128)}) custom-call(bf16[16,576,128]{2,1,0:T(8,128)(2,1)} %bitcast.6, bf16[576,128]{1,0:T(8,128)(2,1)} %bitcast.7, s32[1,128]{1,0:T(1,128)} %bitcast.8, bf16[512,16,128]{2,1,0:T(8,128)(2,1)} %vup_hbm.1, ...), custom_call_target="tpu_custom_call" | custom-call | tf_op jit(solution)/shard_map/pallas_call | solution.py:713
  86.2 3.4 %shard_map.85 = (bf16[128,16,128]{2,1,0:T(8,128)(2,1)}, bf16[16,576,128]{2,1,0:T(8,128)(2,1)}, bf16[576,128]{1,0:T(8,128)(2,1)}, f32[128,128]{1,0:T(8,128)}) custom-call(bf16[128,16,128]{2,1,0:T(8,128)(2,1)} %get-tuple-element.12.attn, bf16[16,576,128]{2,1,0:T(8,128)(2,1)} %get-tuple-element.13.gq, bf16[576,128]{1,0:T(8,128)(2,1)} %get-tuple-element.14.gl, ...), custom_call_target="tpu_custom_call" | custom-call | tf_op jit(solution)/shard_map/pallas_call | solution.py:753
